TPU v7x, 32 devices: a whole 2x2x4 slice. The times are simulated.
32 devices in a mesh: seq: 4 (over y, core), fsdp: 8 (over z, x).
Axes of the slice: x: 2, y: 2, z: 4, core: 2. Of those that a mesh axis runs over, the one named last changes fastest.
Arguments:
- inputs: bfloat16 [8, 1024, 640], P('fsdp', 'seq'), may hold values from -6 to 6
- cotangent: bfloat16 [8, 1024, 640], P('fsdp', 'seq'), may hold values from -6 to 6
- query_proj: bfloat16 [640, 1024], P('fsdp'), may hold values from -0.25 to 0.25
- key_proj: bfloat16 [640, 256], P('fsdp'), may hold values from -0.25 to 0.25
- value_proj: bfloat16 [640, 256], P('fsdp'), may hold values from -0.25 to 0.25
- output_proj: bfloat16 [1024, 640], P('fsdp'), may hold values from -0.1875 to 0.1875
- gate_proj: bfloat16 [640, 2048], P('fsdp'), may hold values from -0.25 to 0.25
- up_proj: bfloat16 [640, 2048], P('fsdp'), may hold values from -0.25 to 0.25
- down_proj: bfloat16 [2048, 640], P('fsdp'), may hold values from -0.125 to 0.125
- attn_norm: bfloat16 [640], P('fsdp'), may hold values from 0.5 to 1.5
- attn_post_norm: bfloat16 [640], P('fsdp'), may hold values from 0.5 to 1.5
- ffn_norm: bfloat16 [640], P('fsdp'), may hold values from 0.5 to 1.5
- ffn_post_norm: bfloat16 [640], P('fsdp'), may hold values from 0.5 to 1.5
- query_norm: bfloat16 [256], P('fsdp'), may hold values from 0.5 to 1.5
- key_norm: bfloat16 [256], P('fsdp'), may hold values from 0.5 to 1.5
Outputs:
- outputs: bfloat16 [8, 1024, 640], P('fsdp', 'seq')
- input_grad: bfloat16 [8, 1024, 640], P('fsdp', 'seq')
- query_proj_grad: float32 [640, 1024], P('fsdp')
- key_proj_grad: float32 [640, 256], P('fsdp')
- value_proj_grad: float32 [640, 256], P('fsdp')
- output_proj_grad: float32 [1024, 640], P('fsdp')
- gate_proj_grad: float32 [640, 2048], P('fsdp')
- up_proj_grad: float32 [640, 2048], P('fsdp')
- down_proj_grad: float32 [2048, 640], P('fsdp')
- attn_norm_grad: float32 [640], P('fsdp')
- attn_post_norm_grad: float32 [640], P('fsdp')
- ffn_norm_grad: float32 [640], P('fsdp')
- ffn_post_norm_grad: float32 [640], P('fsdp')
- query_norm_grad: float32 [256], P('fsdp')
- key_norm_grad: float32 [256], P('fsdp')
All inputs are finite; a program needn't handle non-finite values.
Results may differ from a plain program's by a relative error of at most 0.017.
Values may be sent and summed in bfloat16 or wider, within the bound.
A program may use at most 128 MiB of HBM per device.

v0:
```python
import jax
import jax.numpy as jnp
from jax import lax
from jax.sharding import PartitionSpec as P

WINDOW = 512


eps = 1e-06
base_rate = 10000.0


def shifted(array, axis, by):
    size = lax.axis_size(axis)
    pairs = [(i, i + by) for i in range(size) if 0 <= i + by < size]
    return lax.ppermute(array, axis, pairs)


def rms_scale(value, gain):
    return value * lax.rsqrt(jnp.mean(value * value, axis=-1, keepdims=True) + eps) * gain


def rope_tables(positions, head_width):
    half_width = head_width // 2
    frequency = base_rate ** (-jnp.arange(half_width, dtype=jnp.float32) * 2.0 / head_width)
    angles = positions.astype(jnp.float32)[:, None] * frequency[None, :]
    return (jnp.cos(angles), jnp.sin(angles))


def rotate(value, cos_table, sin_table):
    half_width = value.shape[-1] // 2
    first_half = value[..., :half_width]
    second = value[..., half_width:]
    return jnp.concatenate(
        [first_half * cos_table - second * sin_table, second * cos_table + first_half * sin_table],
        axis=-1,
    )


def row_outer(left, right):
    return lax.dot_general(
        left, right, (((0,), (0,)), ((), ())), preferred_element_type=jnp.float32
    )


def back_product(grad_rows, weight):
    return lax.dot_general(
        grad_rows, weight, (((1,), (1,)), ((), ())), preferred_element_type=jnp.float32
    )


def unpack(gathered):
    matrices = gathered[:7]
    gains = tuple((member.astype(jnp.float32) for member in gathered[7:]))
    return (matrices, gains)


def on_device(
    inputs,
    cotangent,
    query_proj,
    key_proj,
    value_proj,
    output_proj,
    gate_proj,
    up_proj,
    down_proj,
    attn_norm,
    attn_post_norm,
    ffn_norm,
    ffn_post_norm,
    query_norm,
    key_norm,
):
    gathered = (
        lax.all_gather(query_proj, "fsdp", axis=0, tiled=True),
        lax.all_gather(key_proj, "fsdp", axis=0, tiled=True),
        lax.all_gather(value_proj, "fsdp", axis=0, tiled=True),
        lax.all_gather(output_proj, "fsdp", axis=0, tiled=True),
        lax.all_gather(gate_proj, "fsdp", axis=0, tiled=True),
        lax.all_gather(up_proj, "fsdp", axis=0, tiled=True),
        lax.all_gather(down_proj, "fsdp", axis=0, tiled=True),
        lax.all_gather(attn_norm, "fsdp", axis=0, tiled=True),
        lax.all_gather(attn_post_norm, "fsdp", axis=0, tiled=True),
        lax.all_gather(ffn_norm, "fsdp", axis=0, tiled=True),
        lax.all_gather(ffn_post_norm, "fsdp", axis=0, tiled=True),
        lax.all_gather(query_norm, "fsdp", axis=0, tiled=True),
        lax.all_gather(key_norm, "fsdp", axis=0, tiled=True),
    )
    matrices, gains = unpack(gathered)
    query_w, key_w, value_w, output_w, gate_w, up_w, down_w = matrices
    attn_gain, attn_post_gain, ffn_gain, ffn_post_gain, query_gain, key_gain = gains
    source = inputs[0].astype(jnp.float32)
    tokens = source.shape[0]
    head_width = key_w.shape[1]
    head_count = query_w.shape[1] // head_width
    score_scale = head_width ** (-0.5)
    hop_count = min((WINDOW + tokens - 2) // tokens, lax.axis_size("seq") - 1)
    seq_place = lax.axis_index("seq")
    positions = seq_place * tokens + jnp.arange(tokens, dtype=jnp.int32)
    cos_table, sin_table = rope_tables(positions, head_width)
    normed = rms_scale(source, attn_gain).astype(jnp.bfloat16)
    query_raw = jnp.dot(normed, query_w, preferred_element_type=jnp.float32)
    key_raw = jnp.dot(normed, key_w, preferred_element_type=jnp.float32)
    value_raw = jnp.dot(normed, value_w, preferred_element_type=jnp.float32)

    def turn_norm(query_in, key_in, q_gain, k_gain):
        query_out = rotate(
            rms_scale(query_in.reshape(tokens, head_count, head_width), q_gain),
            cos_table[:, None, :],
            sin_table[:, None, :],
        )
        key_out = rotate(rms_scale(key_in, k_gain), cos_table, sin_table)
        return (query_out, key_out)

    query_rot, key_rot = turn_norm(query_raw, key_raw, query_gain, key_gain)
    query_low = query_rot.astype(jnp.bfloat16)
    own_pairs = jnp.concatenate(
        [key_rot.astype(jnp.bfloat16), value_raw.astype(jnp.bfloat16)], axis=1
    )
    received = []
    for distance in range(1, hop_count + 1):
        received.append(shifted(own_pairs, "seq", distance))
    key_value = jnp.concatenate(received[::-1] + [own_pairs], axis=0)
    keys_ext = key_value[:, :head_width]
    values_ext = key_value[:, head_width:]
    ext_rows = key_value.shape[0]
    key_pos = (seq_place - hop_count) * tokens + jnp.arange(ext_rows, dtype=jnp.int32)
    offset = positions[:, None] - key_pos[None, :]
    allowed = ((offset >= 0) & (offset < WINDOW) & (key_pos[None, :] >= 0))[None]
    scores = (
        jnp.einsum("qhd,kd->hqk", query_low, keys_ext, preferred_element_type=jnp.float32)
        * score_scale
    )
    masked = jnp.where(allowed, scores, -1e30)
    row_max = jnp.max(masked, axis=-1, keepdims=True)
    raised = jnp.exp(masked - row_max)
    row_sum = jnp.sum(raised, axis=-1, keepdims=True)
    attn_prob = raised / row_sum
    log_total = row_max + jnp.log(row_sum)
    attended = jnp.einsum(
        "hqk,kd->qhd",
        attn_prob.astype(jnp.bfloat16),
        values_ext,
        preferred_element_type=jnp.float32,
    )
    att_low = attended.reshape(tokens, head_count * head_width).astype(jnp.bfloat16)
    branch = jnp.dot(att_low, output_w, preferred_element_type=jnp.float32)
    middle = source + rms_scale(branch, attn_post_gain)
    normed2 = rms_scale(middle, ffn_gain).astype(jnp.bfloat16)
    gate_val = jnp.dot(normed2, gate_w, preferred_element_type=jnp.float32)
    upper = jnp.dot(normed2, up_w, preferred_element_type=jnp.float32)

    def act_piece(gate_in, upper_in):
        return jax.nn.gelu(gate_in, approximate=True) * upper_in

    hidden = act_piece(gate_val, upper).astype(jnp.bfloat16)
    down_out = jnp.dot(hidden, down_w, preferred_element_type=jnp.float32)
    result = middle + rms_scale(down_out, ffn_post_gain)
    regathered = (
        lax.all_gather(query_proj, "fsdp", axis=0, tiled=True),
        lax.all_gather(key_proj, "fsdp", axis=0, tiled=True),
        lax.all_gather(value_proj, "fsdp", axis=0, tiled=True),
        lax.all_gather(output_proj, "fsdp", axis=0, tiled=True),
        lax.all_gather(gate_proj, "fsdp", axis=0, tiled=True),
        lax.all_gather(up_proj, "fsdp", axis=0, tiled=True),
        lax.all_gather(down_proj, "fsdp", axis=0, tiled=True),
        lax.all_gather(attn_norm, "fsdp", axis=0, tiled=True),
        lax.all_gather(attn_post_norm, "fsdp", axis=0, tiled=True),
        lax.all_gather(ffn_norm, "fsdp", axis=0, tiled=True),
        lax.all_gather(ffn_post_norm, "fsdp", axis=0, tiled=True),
        lax.all_gather(query_norm, "fsdp", axis=0, tiled=True),
        lax.all_gather(key_norm, "fsdp", axis=0, tiled=True),
    )
    matrices, gains = unpack(regathered)
    query_w, key_w, value_w, output_w, gate_w, up_w, down_w = matrices
    attn_gain, attn_post_gain, ffn_gain, ffn_post_gain, query_gain, key_gain = gains
    grad_y = cotangent[0].astype(jnp.float32)
    _, back_post2 = jax.vjp(rms_scale, down_out, ffn_post_gain)
    grad_down, grad_post2 = back_post2(grad_y)
    grad_down_low = grad_down.astype(jnp.bfloat16)
    down_grad = row_outer(hidden, grad_down_low)
    grad_hidden = back_product(grad_down_low, down_w)
    _, back_act = jax.vjp(act_piece, gate_val, upper)
    grad_gate, grad_up = back_act(grad_hidden)
    grad_gate_low = grad_gate.astype(jnp.bfloat16)
    grad_up_low = grad_up.astype(jnp.bfloat16)
    gate_grad = row_outer(normed2, grad_gate_low)
    up_grad = row_outer(normed2, grad_up_low)
    grad_normed2 = back_product(grad_gate_low, gate_w) + back_product(grad_up_low, up_w)
    _, back_pre2 = jax.vjp(rms_scale, middle, ffn_gain)
    grad_mid_norm, grad_pre2 = back_pre2(grad_normed2)
    grad_mid = grad_y + grad_mid_norm
    _, back_post1 = jax.vjp(rms_scale, branch, attn_post_gain)
    grad_branch, grad_post1 = back_post1(grad_mid)
    grad_branch_low = grad_branch.astype(jnp.bfloat16)
    output_grad = row_outer(att_low, grad_branch_low)
    grad_att = (
        back_product(grad_branch_low, output_w)
        .astype(jnp.bfloat16)
        .reshape(tokens, head_count, head_width)
    )
    scores_again = (
        jnp.einsum("qhd,kd->hqk", query_low, keys_ext, preferred_element_type=jnp.float32)
        * score_scale
    )
    prob_again = jnp.exp(jnp.where(allowed, scores_again, -1e30) - log_total)
    grad_prob = jnp.einsum("qhd,kd->hqk", grad_att, values_ext, preferred_element_type=jnp.float32)
    inner_sum = jnp.sum(prob_again * grad_prob, axis=-1, keepdims=True)
    grad_scores = (prob_again * (grad_prob - inner_sum)).astype(jnp.bfloat16)
    grad_query = (
        jnp.einsum("hqk,kd->qhd", grad_scores, keys_ext, preferred_element_type=jnp.float32)
        * score_scale
    )
    grad_keys_ext = (
        jnp.einsum("hqk,qhd->kd", grad_scores, query_low, preferred_element_type=jnp.float32)
        * score_scale
    )
    grad_values_ext = jnp.einsum(
        "hqk,qhd->kd", prob_again.astype(jnp.bfloat16), grad_att, preferred_element_type=jnp.float32
    )
    grad_pairs = jnp.concatenate([grad_keys_ext, grad_values_ext], axis=1)
    own_grad = grad_pairs[hop_count * tokens :]
    for distance in range(1, hop_count + 1):
        lower_row = (hop_count - distance) * tokens
        own_grad = own_grad + shifted(grad_pairs[lower_row : lower_row + tokens], "seq", -distance)
    _, back_turn = jax.vjp(turn_norm, query_raw, key_raw, query_gain, key_gain)
    grad_qraw, grad_kraw, grad_qgain, grad_kgain = back_turn((grad_query, own_grad[:, :head_width]))
    grad_qraw_low = grad_qraw.astype(jnp.bfloat16)
    grad_kraw_low = grad_kraw.astype(jnp.bfloat16)
    grad_vraw_low = own_grad[:, head_width:].astype(jnp.bfloat16)
    query_grad = row_outer(normed, grad_qraw_low)
    key_grad = row_outer(normed, grad_kraw_low)
    value_grad = row_outer(normed, grad_vraw_low)
    grad_normed = (
        back_product(grad_qraw_low, query_w)
        + back_product(grad_kraw_low, key_w)
        + back_product(grad_vraw_low, value_w)
    )
    _, back_pre1 = jax.vjp(rms_scale, source, attn_gain)
    grad_source, grad_pre1 = back_pre1(grad_normed)
    grad_input = grad_mid + grad_source
    shares = (
        lax.psum_scatter(query_grad, "fsdp", scatter_dimension=0, tiled=True),
        lax.psum_scatter(key_grad, "fsdp", scatter_dimension=0, tiled=True),
        lax.psum_scatter(value_grad, "fsdp", scatter_dimension=0, tiled=True),
        lax.psum_scatter(output_grad, "fsdp", scatter_dimension=0, tiled=True),
        lax.psum_scatter(gate_grad, "fsdp", scatter_dimension=0, tiled=True),
        lax.psum_scatter(up_grad, "fsdp", scatter_dimension=0, tiled=True),
        lax.psum_scatter(down_grad, "fsdp", scatter_dimension=0, tiled=True),
        lax.psum_scatter(grad_pre1, "fsdp", scatter_dimension=0, tiled=True),
        lax.psum_scatter(grad_post1, "fsdp", scatter_dimension=0, tiled=True),
        lax.psum_scatter(grad_pre2, "fsdp", scatter_dimension=0, tiled=True),
        lax.psum_scatter(grad_post2, "fsdp", scatter_dimension=0, tiled=True),
        lax.psum_scatter(grad_qgain, "fsdp", scatter_dimension=0, tiled=True),
        lax.psum_scatter(grad_kgain, "fsdp", scatter_dimension=0, tiled=True),
    )
    totals = lax.psum(
        (
            shares[0],
            shares[1],
            shares[2],
            shares[3],
            shares[4],
            shares[5],
            shares[6],
            shares[7],
            shares[8],
            shares[9],
            shares[10],
            shares[11],
            shares[12],
        ),
        "seq",
    )
    return (
        result.astype(jnp.bfloat16)[None],
        grad_input.astype(jnp.bfloat16)[None],
        totals[0],
        totals[1],
        totals[2],
        totals[3],
        totals[4],
        totals[5],
        totals[6],
        totals[7],
        totals[8],
        totals[9],
        totals[10],
        totals[11],
        totals[12],
    )


def solution(mesh):
    placed = (
        P("fsdp", "seq", None),
        P("fsdp", "seq", None),
        P("fsdp", None),
        P("fsdp", None),
        P("fsdp", None),
        P("fsdp", None),
        P("fsdp", None),
        P("fsdp", None),
        P("fsdp", None),
        P("fsdp"),
        P("fsdp"),
        P("fsdp"),
        P("fsdp"),
        P("fsdp"),
        P("fsdp"),
    )
    return jax.shard_map(
        on_device,
        mesh=mesh,
        in_specs=placed,
        out_specs=(
            P("fsdp", "seq", None),
            P("fsdp", "seq", None),
            P("fsdp", None),
            P("fsdp", None),
            P("fsdp", None),
            P("fsdp", None),
            P("fsdp", None),
            P("fsdp", None),
            P("fsdp", None),
            P("fsdp"),
            P("fsdp"),
            P("fsdp"),
            P("fsdp"),
            P("fsdp"),
            P("fsdp"),
        ),
        check_vma=False,
    )
```

profile of v0, /device:TPU:0, one launch (start us, length us, event | category | flops | bytes accessed | tf_op | source)
XLA Modules:
  0.0 982.8 jit_solution(17657719149670648951)
XLA Ops:
  10.0 1.3 fusion.91
  17.7 23.7 %all-reduce.19 = (bf16[640]{0:T(1024)(128)(2,1)S(1)}, bf16[256]{0:T(256)(128)(2,1)S(1)}, bf16[256]{0:T(256)(128)(2,1)S(1)}, bf16[640]{0:T(1024)(128)(2,1)S(1)}, ...) all-reduce(bf16[640]{0:T(1024)(128)(2,1)S(1)} %dynamic-update-slice, ...), channel_id=1, replica_groups=mesh['seq'=4,'fsdp'=8] {'fsdp'}, use_global_device_ids=true, to_apply=%add.4 | all-reduce | flops 3072 | bytes 12288
  42.6 31.2 %all_gather.53 = bf16[640,256]{1,0:T(8,128)(2,1)S(1)} all-gather(bf16[80,256]{1,0:T(8,128)(2,1)} %param.18), channel_id=1, replica_groups=mesh['seq'=4,'fsdp'=8] {'fsdp'}, dimensions={0}, use_global_device_ids=true | all-gather | bytes 368640 | tf_op jit(solution)/shard_map/all_gather | solution.py:77
  73.8 31.9 %all_gather.55 = bf16[640,256]{1,0:T(8,128)(2,1)S(1)} all-gather(bf16[80,256]{1,0:T(8,128)(2,1)} %param.19), channel_id=1, replica_groups=mesh['seq'=4,'fsdp'=8] {'fsdp'}, dimensions={0}, use_global_device_ids=true | all-gather | bytes 368640 | tf_op jit(solution)/shard_map/all_gather | solution.py:78
  108.0 1.3 collective-permute-start.1
  109.3 4.1 collective-permute-start
  114.7 5.5 collective-permute-done
  121.1 1.7 copy.40
  126.4 1.5 fusion.17
  128.0 2.2 multiply_reduce_fusion.9
  133.0 24.6 %all-gather.10.cloned.1.call-done = bf16[640,2048]{1,0:T(8,128)(2,1)} async-done(((bf16[80,2048]{1,0:T(8,128)(2,1)}), bf16[640,2048]{1,0:T(8,128)(2,1)}) %all-gather.10.cloned.1.call-update) | async-done | bytes 2621456 | tf_op jit(solution)/shard_map/all_gather | solution.py:80
  157.6 4.2 fusion.93
  161.8 51.1 %all-gather.12.cloned.1.call-done = bf16[640,2048]{1,0:T(8,128)(2,1)} async-done(((bf16[80,2048]{1,0:T(8,128)(2,1)}), bf16[640,2048]{1,0:T(8,128)(2,1)}) %all-gather.12.cloned.1.call-update) | async-done | bytes 2621456 | tf_op jit(solution)/shard_map/all_gather | solution.py:81
  212.9 5.3 multiply_convert_fusion.1
  218.2 50.0 %all-gather.14.cloned.1.call-done = bf16[2048,640]{1,0:T(8,128)(2,1)} async-done(((bf16[256,640]{1,0:T(8,128)(2,1)}), bf16[2048,640]{1,0:T(8,128)(2,1)}) %all-gather.14.cloned.1.call-update) | async-done | bytes 2621456 | tf_op jit(solution)/shard_map/all_gather | solution.py:82
  268.2 3.3 multiply_reduce_fusion.7
  273.2 2.5 multiply_convert_fusion
  277.1 1.2 copy-done.24
  278.3 1.2 multiply_reduce_fusion.3
  281.6 1.4 convolution_convert_fusion
  283.0 2.0 copy.59
  285.1 1.8 fusion.18
  289.8 1.3 collective-permute-start.2
  291.2 1.4 collective-permute-start.3
  293.6 18.0 %collective-permute-done.3 = f32[256,512]{0,1:T(8,128)S(1)} collective-permute-done((f32[256,512]{0,1:T(8,128)S(1)}, f32[256,512]{0,1:T(8,128)S(1)}, u32[]{:S(2)}, u32[]{:S(2)}) %collective-permute-start.3) | collective-permute-done | bytes 524320 | tf_op jit(solution)/shard_map/ppermute | solution.py:16
  311.7 1.2 fusion.74
  314.6 1.2 fusion.85
  315.9 2.1 fusion.96
  318.0 1.3 copy-done.9
  319.4 1.6 fusion.16
  321.7 2.1 fusion.54
  325.2 3.2 fusion.98
  329.6 3.2 fusion.97
  334.1 3.4 fusion.99
  337.6 35.2 %reduce-scatter.12.cloned.1.call-done = f32[80,256]{1,0:T(8,128)} async-done(((f32[640,256]{1,0:T(8,128)}), f32[80,256]{1,0:T(8,128)}) %reduce-scatter.12.cloned.1.call-update) | async-done | bytes 81936 | tf_op jit(solution)/shard_map/reduce_scatter | solution.py:246
  372.8 65.4 %reduce-scatter.10.cloned.1.call-done = f32[80,256]{1,0:T(8,128)} async-done(((f32[640,256]{1,0:T(8,128)}), f32[80,256]{1,0:T(8,128)}) %reduce-scatter.10.cloned.1.call-update) | async-done | bytes 81936 | tf_op jit(solution)/shard_map/reduce_scatter | solution.py:245
  438.2 72.9 %reduce-scatter.14.cloned.1.call-done = f32[128,640]{1,0:T(8,128)} async-done(((f32[1024,640]{1,0:T(8,128)}), f32[128,640]{1,0:T(8,128)}) %reduce-scatter.14.cloned.1.call-update) | async-done | bytes 327696 | tf_op jit(solution)/shard_map/reduce_scatter | solution.py:247
  511.2 72.9 %reduce-scatter.8.cloned.1.call-done = f32[80,1024]{1,0:T(8,128)} async-done(((f32[640,1024]{1,0:T(8,128)}), f32[80,1024]{1,0:T(8,128)}) %reduce-scatter.8.cloned.1.call-update) | async-done | bytes 327696 | tf_op jit(solution)/shard_map/reduce_scatter | solution.py:244
  584.1 104.9 %reduce-scatter.18.cloned.1.call-done = f32[80,2048]{1,0:T(8,128)} async-done(((f32[640,2048]{1,0:T(8,128)}), f32[80,2048]{1,0:T(8,128)}) %reduce-scatter.18.cloned.1.call-update) | async-done | bytes 655376 | tf_op jit(solution)/shard_map/reduce_scatter | solution.py:249
  689.0 105.9 %reduce-scatter.16.cloned.1.call-done = f32[80,2048]{1,0:T(8,128)} async-done(((f32[640,2048]{1,0:T(8,128)}), f32[80,2048]{1,0:T(8,128)}) %reduce-scatter.16.cloned.1.call-update) | async-done | bytes 655376 | tf_op jit(solution)/shard_map/reduce_scatter | solution.py:248
  794.9 105.8 %reduce-scatter.20.cloned.1.call-done = f32[256,640]{1,0:T(8,128)} async-done(((f32[2048,640]{1,0:T(8,128)}), f32[256,640]{1,0:T(8,128)}) %reduce-scatter.20.cloned.1.call-update) | async-done | bytes 655376 | tf_op jit(solution)/shard_map/reduce_scatter | solution.py:250
  903.4 35.9 %all-reduce.16 = (f32[640]{0:T(1024)S(1)}, f32[640]{0:T(1024)S(1)}, f32[640]{0:T(1024)S(1)}, f32[640]{0:T(1024)S(1)}, f32[256]{0:T(256)S(1)}, /*index=5*/f32[256]{0:T(256)S(1)}) all-reduce(f32[640]{0:T(1024)S(1)} %get-tuple-element.23, f32[640]{0:T(1024)S(1)} %get-tuple-element.19, ...), channel_id=9, replica_groups=mesh['seq'=4,'fsdp'=8] {'fsdp'}, use_global_device_ids=true, to_apply=%region_30.31.clone | all-reduce | flops 3072 | bytes 24576
  939.8 6.6 all-reduce.17
  947.3 19.8 %all-reduce.22.cloned.1.call-done = (f32[80,1024]{1,0:T(8,128)}, f32[80,256]{1,0:T(8,128)}, f32[80,256]{1,0:T(8,128)}, f32[128,640]{1,0:T(8,128)}, f32[80,2048]{...) async-done(((f32[80,1024]{1,0:T(8,128)}, f32[80,256]{1,0:T(8,128)}, f32[80,256]{1,0:T(8,128)}, f32[128,640]{1,0:T(8,128)}, f32[80,2048]{1,0:T(8,128)}, ...) | async-done | bytes 2785296 | tf_op jit(solution)/shard_map/psum | solution.py:258
  967.1 1.9 copy.73
  969.0 1.5 copy.74
  970.5 1.5 copy.75
  972.0 1.7 copy.76
  (218 shorter events, 40.4 us)
Async XLA Ops:
  7.2 98.5 %copy-start = (bf16[1,256,640]{2,1,0:T(8,128)(2,1)S(1)}, bf16[1,256,640]{2,1,0:T(8,128)(2,1)}, u32[]{:S(2)}) copy-start(bf16[1,256,640]{2,1,0:T(8,128)(2,1)} %param.15) | copy-start | bytes 983044
  7.2 113.9 %all-gather.6.cloned.1.call-start = ((), (), s32[]{:S(2)}) async-start(), calls=%async_computation.7 | async-start | bytes 1474560 | tf_op jit(solution)/shard_map/all_gather | solution.py:76
  7.9 120.0 %all-gather.8.cloned.1.call-start = ((), (), s32[]{:S(2)}) async-start(), calls=%async_computation.8 | async-start | bytes 1474560 | tf_op jit(solution)/shard_map/all_gather | solution.py:79
  8.7 148.9 %all-gather.10.cloned.1.call-start = ((), (), s32[]{:S(2)}) async-start(), calls=%async_computation.9 | async-start | bytes 2949120 | tf_op jit(solution)/shard_map/all_gather | solution.py:80
  9.4 203.5 %all-gather.12.cloned.1.call-start = ((), (), s32[]{:S(2)}) async-start(), calls=%async_computation.10 | async-start | bytes 2949120 | tf_op jit(solution)/shard_map/all_gather | solution.py:81
  10.0 258.2 %all-gather.14.cloned.1.call-start = ((), (), s32[]{:S(2)}) async-start(), calls=%async_computation.11 | async-start | bytes 2949120 | tf_op jit(solution)/shard_map/all_gather | solution.py:82
  41.4 66.5 %copy-start.51 = (f32[128]{0:T(128)}, f32[128]{0:T(128)S(1)}, u32[]{:S(2)}) copy-start(f32[128]{0:T(128)S(1)} %multiply_power_fusion) | copy-start | bytes 1540
  73.8 34.1 %copy-start.33 = (bf16[640,256]{1,0:T(8,128)(2,1)}, bf16[640,256]{1,0:T(8,128)(2,1)S(1)}, u32[]{:S(2)}) copy-start(bf16[640,256]{1,0:T(8,128)(2,1)S(1)} %all_gather.53) | copy-start | bytes 983044
  105.7 1.8 copy-start.31
  107.5 16.3 %copy-start.35 = (f32[256,128]{0,1:T(8,128)}, f32[256,128]{0,1:T(8,128)S(1)}, u32[]{:S(2)}) copy-start(f32[256,128]{0,1:T(8,128)S(1)} %get-tuple-element.69) | copy-start | bytes 393220
  107.5 16.3 %copy-start.37 = (f32[256,128]{0,1:T(8,128)}, f32[256,128]{0,1:T(8,128)S(1)}, u32[]{:S(2)}) copy-start(f32[256,128]{0,1:T(8,128)S(1)} %get-tuple-element.70) | copy-start | bytes 393220
  108.0 6.7 collective-permute-start.1
  109.3 10.9 %collective-permute-start = (bf16[256,512]{0,1:T(8,128)(2,1)S(1)}, bf16[256,512]{0,1:T(8,128)(2,1)S(1)}, u32[]{:S(2)}, u32[]{:S(2)}) collective-permute-start(bf16[256,512]{0,1:T(8,128)(2,1)S(1)} %pad_maximum_fusion.4), channel_id=1, source_target_pairs={{0,16},{8,24},{1,17},{9,25},{2,18},{10,26},{3,19},{11,27},{4,20},{... | collective-permute-start | bytes 786440 | tf_op jit(solution)/shard_map/ppermute | solution.py:16
  113.5 259.3 %reduce-scatter.12.cloned.1.call-start = ((), (), s32[]{:S(2)}) async-start(), calls=%async_computation.14 | async-start | bytes 737280 | tf_op jit(solution)/shard_map/reduce_scatter | solution.py:246
  124.0 2.0 copy-start.46
  124.0 2.0 copy-start.48
  268.2 3.3 copy-start.19
  268.2 3.6 copy-start.4
  268.2 4.6 copy-start.53
  268.2 4.6 copy-start.54
  271.4 1.8 copy-start.27
  272.8 3.0 copy-start.29
  273.2 2.5 copy-start.23
  275.8 2.5 copy-start.24
  279.5 2.1 copy-start.13
  285.1 1.8 copy-start.14
  285.1 1.8 copy-start.18
  289.8 3.8 collective-permute-start.2
  291.1 21.9 %copy-start.52 = (f32[128]{0:T(128)S(1)}, f32[128]{0:T(128)}, u32[]{:S(2)}) copy-start(f32[128]{0:T(128)} %copy-done.51) | copy-start | bytes 1540
  291.1 22.4 %copy-start.26 = (f32[256,256]{0,1:T(8,128)S(1)}, f32[256,256]{0,1:T(8,128)}, u32[]{:S(2)}) copy-start(f32[256,256]{0,1:T(8,128)} %copy-done.25) | copy-start | bytes 786436
  291.2 20.4 %collective-permute-start.3 = (f32[256,512]{0,1:T(8,128)S(1)}, f32[256,512]{0,1:T(8,128)S(1)}, u32[]{:S(2)}, u32[]{:S(2)}) collective-permute-start(f32[256,512]{0,1:T(8,128)S(1)} %get-tuple-element.58), channel_id=1, source_target_pairs={{16,0},{24,8},{17,1},{25,9},{18,2},{26,10},{19,3},{27,11},{20,4},{... | collective-permute-start | bytes 1572872 | tf_op jit(solution)/shard_map/ppermute | solution.py:16
  312.9 2.9 copy-start.21
  312.9 2.9 copy-start.28
  313.0 125.3 %reduce-scatter.10.cloned.1.call-start = ((), (), s32[]{:S(2)}) async-start(), calls=%async_computation.13 | async-start | bytes 737280 | tf_op jit(solution)/shard_map/reduce_scatter | solution.py:245
  315.8 195.4 %reduce-scatter.14.cloned.1.call-start = ((), (), s32[]{:S(2)}) async-start(), calls=%async_computation.15 | async-start | bytes 2949120 | tf_op jit(solution)/shard_map/reduce_scatter | solution.py:247
  318.0 3.2 copy-start.2
  318.0 266.1 %reduce-scatter.8.cloned.1.call-start = ((), (), s32[]{:S(2)}) async-start(), calls=%async_computation.12 | async-start | bytes 2949120 | tf_op jit(solution)/shard_map/reduce_scatter | solution.py:244
  323.9 365.1 %reduce-scatter.18.cloned.1.call-start = ((), (), s32[]{:S(2)}) async-start(), calls=%async_computation.17 | async-start | bytes 5898240 | tf_op jit(solution)/shard_map/reduce_scatter | solution.py:249
  328.4 466.5 %reduce-scatter.16.cloned.1.call-start = ((), (), s32[]{:S(2)}) async-start(), calls=%async_computation.16 | async-start | bytes 5898240 | tf_op jit(solution)/shard_map/reduce_scatter | solution.py:248
  332.9 567.8 %reduce-scatter.20.cloned.1.call-start = ((), (), s32[]{:S(2)}) async-start(), calls=%async_computation.18 | async-start | bytes 5898240 | tf_op jit(solution)/shard_map/reduce_scatter | solution.py:250
  337.5 564.4 %copy-start.34 = (bf16[640,256]{1,0:T(8,128)(2,1)S(1)}, bf16[640,256]{1,0:T(8,128)(2,1)}, u32[]{:S(2)}) copy-start(bf16[640,256]{1,0:T(8,128)(2,1)} %copy-done.33) | copy-start | bytes 983044
  337.5 564.4 %copy-start.40 = (bf16[256,256]{0,1:T(8,128)(2,1)S(1)}, bf16[256,256]{0,1:T(8,128)(2,1)}, u32[]{:S(2)}) copy-start(bf16[256,256]{0,1:T(8,128)(2,1)} %copy-done.39) | copy-start | bytes 393220
  337.5 564.8 %copy-start.12 = (bf16[640,1024]{1,0:T(8,128)(2,1)S(1)}, bf16[640,1024]{1,0:T(8,128)(2,1)}, u32[]{:S(2)}) copy-start(bf16[640,1024]{1,0:T(8,128)(2,1)} %all-gather.6.cloned.1.call-done) | copy-start | bytes 3932164
  337.6 629.5 %all-reduce.22.cloned.1.call-start = ((), (), s32[]{:S(2)}) async-start(), calls=%async_computation.19 | async-start | bytes 5570560 | tf_op jit(solution)/shard_map/psum | solution.py:258
  902.3 44.1 %copy-start.11 = (f32[256,640]{1,0:T(8,128)S(1)}, f32[256,640]{1,0:T(8,128)}, u32[]{:S(2)}) copy-start(f32[256,640]{1,0:T(8,128)} %copy-done.10) | copy-start | bytes 1966084
  967.1 6.6 copy-start.45
  967.1 7.5 copy-start.44
  967.1 8.3 copy-start.43
  (24 other events, 27.5 us)
Sparse Core Ops, SparseCore 0:
  10.2 46.6 all-gather.5
  59.1 42.6 all-gather.7
  103.9 53.6 all-gather.9
  159.6 53.2 all-gather.11
  214.9 53.2 all-gather.13
  313.1 59.6 reduce-scatter.11
  377.0 61.1 reduce-scatter.9
  441.7 69.3 reduce-scatter.13
  514.7 69.3 reduce-scatter.7
  587.5 101.4 reduce-scatter.17
  692.6 102.2 reduce-scatter.15
  798.3 102.2 reduce-scatter.19
  903.5 63.5 all-reduce.21
where the time goes:
time: 984 us; the launch traced here: 983 us
  waiting for transfers between devices  736 us (75%)
  blocking collectives  129 us (13%)
  matrix products  47.4 us (5%)
  local copies, waits for them, and re-layouts  33.1 us (3%)
  between operations  17.4 us (2%)
  other arithmetic  10.9 us (1%)
    reduce_scatter x1, waiting for transfers between devices, on_device(): lax.psum_scatter(gate_grad, 'fsdp', scatter_dimension=0, tiled=True)  106 us
    reduce_scatter x1, waiting for transfers between devices, on_device(): lax.psum_scatter(down_grad, 'fsdp', scatter_dimension=0, tiled=True)  106 us
    reduce_scatter x1, waiting for transfers between devices, on_device(): lax.psum_scatter(up_grad, 'fsdp', scatter_dimension=0, tiled=True)  105 us
    reduce_scatter x1, waiting for transfers between devices, on_device(): lax.psum_scatter(output_grad, 'fsdp', scatter_dimension=0, tiled=True)  72.9 us
    reduce_scatter x1, waiting for transfers between devices, on_device(): lax.psum_scatter(query_grad, 'fsdp', scatter_dimension=0, tiled=True)  72.9 us
    reduce_scatter x1, waiting for transfers between devices, on_device(): lax.psum_scatter(key_grad, 'fsdp', scatter_dimension=0, tiled=True)  65.4 us
    unnamed x2, blocking collectives  59.6 us
    all_gather x1, waiting for transfers between devices, on_device(): lax.all_gather(up_proj, 'fsdp', axis=0, tiled=True)  51.1 us
  transfers between devices with their start and end apart: 17, of which 14 were waited for; matrix products, arithmetic and copies ran while one was open for 5% of the time, Pallas kernels for 0%

commit v1 on v0

v1 whole, which is shorter than its diff:
```python
import functools

import jax
import jax.numpy as jnp
from jax import lax
from jax.experimental import pallas as pl
from jax.experimental.pallas import tpu as pltpu
from jax.sharding import PartitionSpec as P

WINDOW = 512


eps = 1e-06
base_rate = 10000.0


def shifted(array, axis, by):
    size = lax.axis_size(axis)
    pairs = [(i, i + by) for i in range(size) if 0 <= i + by < size]
    return lax.ppermute(array, axis, pairs)


def rms_scale(value, gain):
    return value * lax.rsqrt(jnp.mean(value * value, axis=-1, keepdims=True) + eps) * gain


def rope_tables(positions, head_width):
    half_width = head_width // 2
    frequency = base_rate ** (-jnp.arange(half_width, dtype=jnp.float32) * 2.0 / head_width)
    angles = positions.astype(jnp.float32)[:, None] * frequency[None, :]
    return (jnp.cos(angles), jnp.sin(angles))


def rotate(value, cos_table, sin_table):
    half_width = value.shape[-1] // 2
    first_half = value[..., :half_width]
    second = value[..., half_width:]
    return jnp.concatenate(
        [first_half * cos_table - second * sin_table, second * cos_table + first_half * sin_table],
        axis=-1,
    )


def row_outer(left, right):
    return lax.dot_general(
        left, right, (((0,), (0,)), ((), ())), preferred_element_type=jnp.float32
    )


def back_product(grad_rows, weight):
    return lax.dot_general(
        grad_rows, weight, (((1,), (1,)), ((), ())), preferred_element_type=jnp.float32
    )


MESH = pl.DeviceIdType.MESH
VMEM_BYTES = 56 * 1024 * 1024


def ring_owner(place, size):
    place = lax.rem(place + 2 * size, size)
    return jnp.where(place < size // 2, 2 * place, 2 * (size - 1 - place) + 1)


def ring_place(owner, size):
    return jnp.where(lax.rem(owner, 2) == 0, owner // 2, size - 1 - owner // 2)


def half_of(shape, by_rows, which):
    rows, columns = shape
    if by_rows:
        size = rows // 2
        return (pl.ds(pl.multiple_of(which * size, size & -size), size), slice(None))
    size = columns // 2
    return (slice(None), pl.ds(pl.multiple_of(which * size, 128), size))


def half_shape(shape, by_rows):
    rows, columns = shape
    return (rows // 2, columns) if by_rows else (rows, columns // 2)


def greet(peers):
    barrier = pltpu.get_barrier_semaphore()
    for peer in peers:
        pl.semaphore_signal(barrier, inc=1, device_id=peer, device_id_type=MESH)
    pl.semaphore_wait(barrier, len(peers))


def gather_kernel(size, shapes, by_rows, *refs):
    count = len(shapes)
    shards, gains = refs[:count], refs[count]
    wholes, all_gains = refs[count + 1 : 2 * count + 1], refs[2 * count + 1]
    own_sem, ring_send, ring_recv, pair_send, pair_recv = refs[2 * count + 2 :]
    seq, me = lax.axis_index("seq"), lax.axis_index("fsdp")
    core = lax.rem(seq, 2)
    way = 1 - 2 * core
    place = ring_place(me, size)
    after = (seq, ring_owner(place + way, size))
    before = (seq, ring_owner(place - way, size))
    pair = (seq + way, me)
    greet([after, before, pair])

    def ring_copy(member, block, step, first=False):
        if member == count:
            source, target = gains if first else all_gains.at[block], all_gains.at[block]
        else:
            part = half_of(shapes[member], by_rows[member], core)
            target = wholes[member].at[(block, *part)]
            source = shards[member].at[part] if first else target
        return pltpu.make_async_remote_copy(
            src_ref=source,
            dst_ref=target,
            send_sem=ring_send.at[step, member],
            recv_sem=ring_recv.at[step, member],
            device_id=after,
            device_id_type=MESH,
        )

    def pair_copy(member, block, step, which):
        part = half_of(shapes[member], by_rows[member], which)
        target = wholes[member].at[(block, *part)]
        return pltpu.make_async_remote_copy(
            src_ref=target,
            dst_ref=target,
            send_sem=pair_send.at[step, member],
            recv_sem=pair_recv.at[step, member],
            device_id=pair,
            device_id_type=MESH,
        )

    own = []
    for member in range(count + 1):
        ring_copy(member, me, 0, first=True).start()
    for member in range(count):
        own.append(
            pltpu.make_async_copy(shards[member], wholes[member].at[me], own_sem.at[member])
        )
    own.append(pltpu.make_async_copy(gains, all_gains.at[me], own_sem.at[count]))
    for copy in own:
        copy.start()

    def arrive(step, forward):
        block = ring_owner(place - way * step, size)
        for member in range(count + 1):
            ring_copy(member, block, step - 1).wait_recv()
            if forward:
                ring_copy(member, block, step).start()
            if member < count:
                pair_copy(member, block, step - 1, core).start()

    lax.fori_loop(1, size - 1, lambda step, _: (arrive(step, True), 0)[1], 0)
    arrive(size - 1, False)
    for copy in own:
        copy.wait()

    def finish(step, _):
        for member in range(count + 1):
            ring_copy(member, me, step).wait_send()
            if member < count:
                pair_copy(member, me, step, core).wait_send()
                block = ring_owner(place + way * (step + 1), size)
                pair_copy(member, block, step, 1 - core).wait_recv()
        return 0

    lax.fori_loop(0, size - 1, finish, 0)


def gather_weights(shards, by_rows, gains):
    size = lax.axis_size("fsdp")
    shapes = [shard.shape for shard in shards]
    count = len(shards)
    any_space = pl.BlockSpec(memory_space=pl.ANY)
    copies = pltpu.SemaphoreType.DMA((size - 1, count + 1))
    return pl.pallas_call(
        functools.partial(gather_kernel, size, shapes, by_rows),
        out_shape=[
            jax.ShapeDtypeStruct((size, *member.shape), member.dtype) for member in (*shards, gains)
        ],
        in_specs=[any_space] * (count + 1),
        out_specs=[any_space] * (count + 1),
        scratch_shapes=[pltpu.SemaphoreType.DMA((count + 1,)), copies, copies, copies, copies],
        compiler_params=pltpu.CompilerParams(collective_id=0, has_side_effects=True),
        name="gather_weights",
    )(*shards, gains)


def reduce_kernel(size, blocks, shapes, by_rows, *refs):
    count = len(shapes)
    every = list(refs)

    def take(number):
        taken = every[:number]
        del every[:number]
        return taken

    mine, (gain_mine,) = take(count), take(1)
    totals, (gain_total,) = take(count), take(1)
    parts, landed, spread = take(count), take(count), take(count)
    gain_sent, gain_landed, gain_spread = take(3)
    pair_send, pair_recv, ring_send, ring_recv = take(4)
    spread_send, spread_recv, gain_send, gain_recv, last_send, last_recv = take(6)

    seq, me = lax.axis_index("seq"), lax.axis_index("fsdp")
    core = lax.rem(seq, 2)
    row = seq // 2
    rows = blocks // 2
    way = 1 - 2 * core
    place = ring_place(me, size)
    after = (seq, ring_owner(place + way, size))
    before = (seq, ring_owner(place - way, size))
    pair = (seq + way, me)
    others = [(lax.rem(seq + by, blocks), me) for by in range(1, blocks)]
    greet([after, before, *others])

    def remote(source, target, send_sem, recv_sem, device):
        return pltpu.make_async_remote_copy(
            src_ref=source,
            dst_ref=target,
            send_sem=send_sem,
            recv_sem=recv_sem,
            device_id=device,
            device_id_type=MESH,
        )

    def pair_copy(member, step):
        block = ring_owner(place + way * (1 + step), size)
        part = half_of(shapes[member], by_rows[member], 1 - core)
        return remote(
            mine[member].at[(block, *part)],
            parts[member].at[block],
            pair_send.at[step, member],
            pair_recv.at[step, member],
            pair,
        )

    def ring_copy(member, step):
        block = ring_owner(place - way * (1 + step), size)
        source = gain_sent.at[step] if member == count else parts[member].at[block]
        target = gain_landed.at[step] if member == count else landed[member].at[step]
        return remote(
            source, target, ring_send.at[step, member], ring_recv.at[step, member], after
        )

    def start_pair(step, _):
        for member in range(count):
            pair_copy(member, step).start()
        return 0

    lax.fori_loop(0, size, start_pair, 0)

    def add_up(step, first, last):
        block = ring_owner(place - way * (1 + step), size)
        for member in range(count):
            pair_copy(member, step).wait_recv()
            part = half_of(shapes[member], by_rows[member], core)
            total = mine[member][(block, *part)].astype(jnp.float32)
            total = total + parts[member][block].astype(jnp.float32)
            if not first:
                ring_copy(member, step - 1).wait_recv()
                total = total + landed[member][step - 1].astype(jnp.float32)
            if last:
                spread[member][row] = total.astype(jnp.bfloat16)
                for by in range(1, rows):
                    spread_copy(member, by).start()
            else:
                parts[member][block] = total.astype(jnp.bfloat16)
                ring_copy(member, step).start()
        total = gain_mine[block]
        if not first:
            ring_copy(count, step - 1).wait_recv()
            total = total + gain_landed[step - 1]
        if last:
            gain_spread[seq] = total
            for by in range(1, blocks):
                gain_copy(by).start()
        else:
            gain_sent[step] = total
            ring_copy(count, step).start()

    def spread_copy(member, by):
        target = spread[member].at[row]
        device = (lax.rem(seq + 2 * by, blocks), me)
        return remote(
            target, target, spread_send.at[by - 1, member], spread_recv.at[by - 1, member], device
        )

    def gain_copy(by):
        target = gain_spread.at[seq]
        return remote(
            target, target, gain_send.at[by - 1], gain_recv.at[by - 1], others[by - 1]
        )

    def last_copy(member):
        target = totals[member].at[half_of(shapes[member], by_rows[member], core)]
        return remote(target, target, last_send.at[member], last_recv.at[member], pair)

    add_up(0, True, False)
    lax.fori_loop(1, size - 1, lambda step, _: (add_up(step, False, False), 0)[1], 0)
    add_up(size - 1, False, True)
    for member in range(count):
        for by in range(1, rows):
            spread_copy(member, by).wait_recv()
        total = spread[member][0].astype(jnp.float32)
        for other in range(1, rows):
            total = total + spread[member][other].astype(jnp.float32)
        totals[member][half_of(shapes[member], by_rows[member], core)] = total
        last_copy(member).start()
    for by in range(1, blocks):
        gain_copy(by).wait_recv()
    total = gain_spread[0]
    for other in range(1, blocks):
        total = total + gain_spread[other]
    gain_total[...] = total

    def finish(step, _):
        for member in range(count + 1):
            ring_copy(member, step).wait_send()
        return 0

    lax.fori_loop(0, size - 1, finish, 0)

    def finish_pair(step, _):
        for member in range(count):
            pair_copy(member, step).wait_send()
        return 0

    lax.fori_loop(0, size, finish_pair, 0)
    for member in range(count):
        for by in range(1, rows):
            spread_copy(member, by).wait_send()
        last_copy(member).wait()
    for by in range(1, blocks):
        gain_copy(by).wait_send()


def reduce_grads(grads, by_rows, gain_grads):
    size, blocks = lax.axis_size("fsdp"), lax.axis_size("seq")
    shapes = [grad.shape[1:] for grad in grads]
    halves = [half_shape(*both) for both in zip(shapes, by_rows)]
    count = len(grads)
    gain_shape = gain_grads.shape[1:]
    rows = blocks // 2
    in_vmem = pl.BlockSpec(memory_space=pltpu.VMEM)
    dma = pltpu.SemaphoreType.DMA
    return pl.pallas_call(
        functools.partial(reduce_kernel, size, blocks, shapes, by_rows),
        out_shape=[jax.ShapeDtypeStruct(shape, jnp.float32) for shape in (*shapes, gain_shape)],
        in_specs=[in_vmem] * (count + 1),
        out_specs=[in_vmem] * (count + 1),
        scratch_shapes=[
            *[pltpu.VMEM((size, *half), jnp.bfloat16) for half in halves],
            *[pltpu.VMEM((size - 1, *half), jnp.bfloat16) for half in halves],
            *[pltpu.VMEM((rows, *half), jnp.bfloat16) for half in halves],
            pltpu.VMEM((size - 1, *gain_shape), jnp.float32),
            pltpu.VMEM((size - 1, *gain_shape), jnp.float32),
            pltpu.VMEM((blocks, *gain_shape), jnp.float32),
            dma((size, count)),
            dma((size, count)),
            dma((size - 1, count + 1)),
            dma((size - 1, count + 1)),
            dma((rows, count)),
            dma((rows, count)),
            dma((blocks,)),
            dma((blocks,)),
            dma((count,)),
            dma((count,)),
        ],
        compiler_params=pltpu.CompilerParams(
            collective_id=1, has_side_effects=True, vmem_limit_bytes=VMEM_BYTES
        ),
        name="reduce_grads",
    )(*grads, gain_grads)


def pack_gains(members, rows, split):
    row = jnp.concatenate([member.reshape(*split, -1) for member in members], axis=-1)
    padding = -row.shape[-1] % 128
    row = jnp.pad(row, [(0, 0)] * len(split) + [(0, padding)])
    return jnp.broadcast_to(row[..., None, :], (*split, rows, row.shape[-1]))


def unpack_gains(rows, widths):
    pieces, start = [], 0
    for width in widths:
        pieces.append(rows[..., start : start + width])
        start += width
    return pieces


def on_device(
    inputs,
    cotangent,
    query_proj,
    key_proj,
    value_proj,
    output_proj,
    gate_proj,
    up_proj,
    down_proj,
    attn_norm,
    attn_post_norm,
    ffn_norm,
    ffn_post_norm,
    query_norm,
    key_norm,
):
    size = lax.axis_size("fsdp")
    shards = (
        jnp.concatenate([query_proj, key_proj, value_proj], axis=1),
        output_proj,
        jnp.concatenate([gate_proj, up_proj], axis=1),
        down_proj,
    )
    by_rows = (False, True, False, True)
    gain_shards = (attn_norm, attn_post_norm, ffn_norm, ffn_post_norm, query_norm, key_norm)
    widths = [member.shape[0] for member in gain_shards]
    *wholes, all_gains = gather_weights(shards, by_rows, pack_gains(gain_shards, 16, ()))
    into_w, output_w, ffn_w, down_w = (whole.reshape(-1, whole.shape[-1]) for whole in wholes)
    query_width, head_width = query_proj.shape[1], key_proj.shape[1]
    ffn_width = gate_proj.shape[1]
    attn_gain, attn_post_gain, ffn_gain, ffn_post_gain, query_gain, key_gain = (
        piece.reshape(-1).astype(jnp.float32) for piece in unpack_gains(all_gains[:, 0], widths)
    )
    source = inputs[0].astype(jnp.float32)
    tokens = source.shape[0]
    head_count = query_width // head_width
    score_scale = head_width ** (-0.5)
    hop_count = min((WINDOW + tokens - 2) // tokens, lax.axis_size("seq") - 1)
    seq_place = lax.axis_index("seq")
    positions = seq_place * tokens + jnp.arange(tokens, dtype=jnp.int32)
    cos_table, sin_table = rope_tables(positions, head_width)
    normed = rms_scale(source, attn_gain).astype(jnp.bfloat16)
    raw = jnp.dot(normed, into_w, preferred_element_type=jnp.float32)
    query_raw = raw[:, :query_width]
    key_raw = raw[:, query_width : query_width + head_width]
    value_raw = raw[:, query_width + head_width :]

    def turn_norm(query_in, key_in, q_gain, k_gain):
        query_out = rotate(
            rms_scale(query_in.reshape(tokens, head_count, head_width), q_gain),
            cos_table[:, None, :],
            sin_table[:, None, :],
        )
        key_out = rotate(rms_scale(key_in, k_gain), cos_table, sin_table)
        return (query_out, key_out)

    query_rot, key_rot = turn_norm(query_raw, key_raw, query_gain, key_gain)
    query_low = query_rot.astype(jnp.bfloat16)
    own_pairs = jnp.concatenate(
        [key_rot.astype(jnp.bfloat16), value_raw.astype(jnp.bfloat16)], axis=1
    )
    received = []
    for distance in range(1, hop_count + 1):
        received.append(shifted(own_pairs, "seq", distance))
    key_value = jnp.concatenate(received[::-1] + [own_pairs], axis=0)
    keys_ext = key_value[:, :head_width]
    values_ext = key_value[:, head_width:]
    ext_rows = key_value.shape[0]
    key_pos = (seq_place - hop_count) * tokens + jnp.arange(ext_rows, dtype=jnp.int32)
    offset = positions[:, None] - key_pos[None, :]
    allowed = ((offset >= 0) & (offset < WINDOW) & (key_pos[None, :] >= 0))[None]
    scores = (
        jnp.einsum("qhd,kd->hqk", query_low, keys_ext, preferred_element_type=jnp.float32)
        * score_scale
    )
    masked = jnp.where(allowed, scores, -1e30)
    row_max = jnp.max(masked, axis=-1, keepdims=True)
    raised = jnp.exp(masked - row_max)
    row_sum = jnp.sum(raised, axis=-1, keepdims=True)
    attn_prob = raised / row_sum
    log_total = row_max + jnp.log(row_sum)
    attended = jnp.einsum(
        "hqk,kd->qhd",
        attn_prob.astype(jnp.bfloat16),
        values_ext,
        preferred_element_type=jnp.float32,
    )
    att_low = attended.reshape(tokens, head_count * head_width).astype(jnp.bfloat16)
    branch = jnp.dot(att_low, output_w, preferred_element_type=jnp.float32)
    middle = source + rms_scale(branch, attn_post_gain)
    normed2 = rms_scale(middle, ffn_gain).astype(jnp.bfloat16)
    both = jnp.dot(normed2, ffn_w, preferred_element_type=jnp.float32)
    gate_val, upper = both[:, :ffn_width], both[:, ffn_width:]

    def act_piece(gate_in, upper_in):
        return jax.nn.gelu(gate_in, approximate=True) * upper_in

    hidden = act_piece(gate_val, upper).astype(jnp.bfloat16)
    down_out = jnp.dot(hidden, down_w, preferred_element_type=jnp.float32)
    result = middle + rms_scale(down_out, ffn_post_gain)
    grad_y = cotangent[0].astype(jnp.float32)
    _, back_post2 = jax.vjp(rms_scale, down_out, ffn_post_gain)
    grad_down, grad_post2 = back_post2(grad_y)
    grad_down_low = grad_down.astype(jnp.bfloat16)
    down_grad = row_outer(hidden, grad_down_low)
    grad_hidden = back_product(grad_down_low, down_w)
    _, back_act = jax.vjp(act_piece, gate_val, upper)
    grad_gate, grad_up = back_act(grad_hidden)
    grad_both = jnp.concatenate(
        [grad_gate.astype(jnp.bfloat16), grad_up.astype(jnp.bfloat16)], axis=1
    )
    ffn_grad = row_outer(normed2, grad_both)
    grad_normed2 = back_product(grad_both, ffn_w)
    _, back_pre2 = jax.vjp(rms_scale, middle, ffn_gain)
    grad_mid_norm, grad_pre2 = back_pre2(grad_normed2)
    grad_mid = grad_y + grad_mid_norm
    _, back_post1 = jax.vjp(rms_scale, branch, attn_post_gain)
    grad_branch, grad_post1 = back_post1(grad_mid)
    grad_branch_low = grad_branch.astype(jnp.bfloat16)
    output_grad = row_outer(att_low, grad_branch_low)
    grad_att = (
        back_product(grad_branch_low, output_w)
        .astype(jnp.bfloat16)
        .reshape(tokens, head_count, head_width)
    )
    scores_again = (
        jnp.einsum("qhd,kd->hqk", query_low, keys_ext, preferred_element_type=jnp.float32)
        * score_scale
    )
    prob_again = jnp.exp(jnp.where(allowed, scores_again, -1e30) - log_total)
    grad_prob = jnp.einsum("qhd,kd->hqk", grad_att, values_ext, preferred_element_type=jnp.float32)
    inner_sum = jnp.sum(prob_again * grad_prob, axis=-1, keepdims=True)
    grad_scores = (prob_again * (grad_prob - inner_sum)).astype(jnp.bfloat16)
    grad_query = (
        jnp.einsum("hqk,kd->qhd", grad_scores, keys_ext, preferred_element_type=jnp.float32)
        * score_scale
    )
    grad_keys_ext = (
        jnp.einsum("hqk,qhd->kd", grad_scores, query_low, preferred_element_type=jnp.float32)
        * score_scale
    )
    grad_values_ext = jnp.einsum(
        "hqk,qhd->kd", prob_again.astype(jnp.bfloat16), grad_att, preferred_element_type=jnp.float32
    )
    grad_pairs = jnp.concatenate([grad_keys_ext, grad_values_ext], axis=1)
    own_grad = grad_pairs[hop_count * tokens :]
    for distance in range(1, hop_count + 1):
        lower_row = (hop_count - distance) * tokens
        own_grad = own_grad + shifted(grad_pairs[lower_row : lower_row + tokens], "seq", -distance)
    _, back_turn = jax.vjp(turn_norm, query_raw, key_raw, query_gain, key_gain)
    grad_qraw, grad_kraw, grad_qgain, grad_kgain = back_turn((grad_query, own_grad[:, :head_width]))
    grad_raw = jnp.concatenate(
        [
            grad_qraw.astype(jnp.bfloat16),
            grad_kraw.astype(jnp.bfloat16),
            own_grad[:, head_width:].astype(jnp.bfloat16),
        ],
        axis=1,
    )
    into_grad = row_outer(normed, grad_raw)
    grad_normed = back_product(grad_raw, into_w)
    _, back_pre1 = jax.vjp(rms_scale, source, attn_gain)
    grad_source, grad_pre1 = back_pre1(grad_normed)
    grad_input = grad_mid + grad_source
    grads = [
        grad.astype(jnp.bfloat16).reshape(size, -1, grad.shape[-1])
        for grad in (into_grad, output_grad, ffn_grad, down_grad)
    ]
    gain_grads = pack_gains(
        (grad_pre1, grad_post1, grad_pre2, grad_post2, grad_qgain, grad_kgain), 8, (size,)
    )
    into_total, output_total, ffn_total, down_total, gain_total = reduce_grads(
        grads, by_rows, gain_grads
    )
    return (
        result.astype(jnp.bfloat16)[None],
        grad_input.astype(jnp.bfloat16)[None],
        into_total[:, :query_width],
        into_total[:, query_width : query_width + head_width],
        into_total[:, query_width + head_width :],
        output_total,
        ffn_total[:, :ffn_width],
        ffn_total[:, ffn_width:],
        down_total,
        *unpack_gains(gain_total[0], widths),
    )


def solution(mesh):
    placed = (
        P("fsdp", "seq", None),
        P("fsdp", "seq", None),
        P("fsdp", None),
        P("fsdp", None),
        P("fsdp", None),
        P("fsdp", None),
        P("fsdp", None),
        P("fsdp", None),
        P("fsdp", None),
        P("fsdp"),
        P("fsdp"),
        P("fsdp"),
        P("fsdp"),
        P("fsdp"),
        P("fsdp"),
    )
    return jax.shard_map(
        on_device,
        mesh=mesh,
        in_specs=placed,
        out_specs=(
            P("fsdp", "seq", None),
            P("fsdp", "seq", None),
            P("fsdp", None),
            P("fsdp", None),
            P("fsdp", None),
            P("fsdp", None),
            P("fsdp", None),
            P("fsdp", None),
            P("fsdp", None),
            P("fsdp"),
            P("fsdp"),
            P("fsdp"),
            P("fsdp"),
            P("fsdp"),
            P("fsdp"),
        ),
        check_vma=False,
    )
```

time: 984 us -> 242 us (0.25)
  waiting for transfers between devices: 736 us -> 17.8 us
  Pallas kernels: 0 us -> 138 us
  blocking collectives: 129 us -> 0 us
  between operations: 17.4 us -> 1.37 us
  matrix products: 47.4 us -> 31.4 us
    reduce_scatter x7 -> x0, waiting for transfers between devices: 563 us -> none  [the longest x1 106 us: on_device(): lax.psum_scatter(gate_grad, 'fsdp', scatter_dimension=0, tiled=True)]
    pallas_call x0 -> x2, Pallas kernels: none -> 138 us  [the longest x1 76.4 us: reduce_grads(): pl.pallas_call(functools.partial(reduce_kernel, size, blocks, shapes, by_...]
    all_gather x5 -> x0, waiting for transfers between devices: 126 us -> none  [the longest x1 51.1 us: on_device(): lax.all_gather(up_proj, 'fsdp', axis=0, tiled=True)]
    all_gather x2 -> x0, blocking collectives: 63.1 us -> none  [the longest x1 31.9 us: on_device(): lax.all_gather(value_proj, 'fsdp', axis=0, tiled=True)]
    unnamed x2 -> x0, blocking collectives: 59.6 us -> none
    unnamed x136 -> x79, local copies, waits for them, and re-layouts: 29.3 us -> 5.97 us
    psum x1 -> x0, waiting for transfers between devices: 19.8 us -> none  [on_device(): lax.psum((shares[0], shares[1], shares[2], shares[3], shares[4], shares[5...]
  transfers between devices with their start and end apart: 17 -> 4, of which waited for: 14 -> 2; matrix products, arithmetic and copies ran while one was open for 5% -> 3% of each run, Pallas kernels for 0% -> 0%
where the time goes in v1:
time: 242 us; the launch traced here: 241 us
  Pallas kernels  138 us (57%)
  matrix products  31.4 us (13%)
  local copies, waits for them, and re-layouts  25.6 us (11%)
  waiting for transfers between devices  17.8 us (7%)
  other arithmetic  17.3 us (7%)
  starting transfers between devices  9.33 us (4%)
    pallas_call x1, Pallas kernels, reduce_grads(): pl.pallas_call(functools.partial(reduce_kernel, size, blocks, shapes, by_...  76.4 us
    pallas_call x1, Pallas kernels, gather_weights(): pl.pallas_call(functools.partial(gather_kernel, size, shapes, by_rows), o...  62.1 us
    ppermute x4, waiting for transfers between devices, shifted(): return lax.ppermute(array, axis, pairs)  17.8 us
    dot_general x4, matrix products, row_outer(): lax.dot_general(left, right, (((0,), (0,)), ((), ())), preferred_element_...  10.3 us
    ppermute x4, starting transfers between devices, shifted(): return lax.ppermute(array, axis, pairs)  9.33 us
    dot_general x4, matrix products, back_product(): lax.dot_general(grad_rows, weight, (((1,), (1,)), ((), ())), preferred_el...  8.17 us
    unnamed x79, local copies, waits for them, and re-layouts  5.97 us
  transfers between devices with their start and end apart: 4, of which 2 were waited for; matrix products, arithmetic and copies ran while one was open for 3% of the time, Pallas kernels for 0%

profile of v1, /device:TPU:0, one launch (start us, length us, event | category | flops | bytes accessed | tf_op | source)
XLA Modules:
  0.0 241.3 jit_solution(10246371654908866289)
XLA Ops:
  0.7 2.0 pad_maximum_fusion.4.refs_2_
  2.7 1.7 pad_maximum_fusion.12.refs_0_
  4.3 4.1 %concatenate.36 = bf16[384]{0:T(512)(128)(2,1)S(1)} concatenate(bf16[80]{0:T(256)(128)(2,1)} %param.24, bf16[80]{0:T(256)(128)(2,1)} %param.25, bf16[80]{0:T(256)(128)(2,1)} %param.26, bf16[80]{0:T(256)(128)(2,1)} %param.27, bf16[32]{0:T(256)(128)(2,1)} %param.28, bf16[32]{0:T(256)(128)(2,1)} %param.29), dimensions={0} | concatenate | bytes 1536 | tf_op jit(solution)/shard_map/concatenate | solution.py:377
  9.0 62.1 %gather_weights.1 = (bf16[8,80,1536]{2,1,0:T(8,128)(2,1)}, bf16[8,128,640]{2,1,0:T(8,128)(2,1)}, bf16[8,80,4096]{2,1,0:T(8,128)(2,1)}, bf16[8,256,640]{2,1,0:T(8,128)(2,1)}, bf16[8,16,384]{2,1,0:T(8,128)(2,1)}) custom-call(bf16[80,1536]{1,0:T(8,128)(2,1)} %pad_maximum_fusion.12.refs_0_, bf16[128,640]{1,0:T(8,128)(2,1)} %refs_1_.1, ...), custom_call_target="tpu_custom_call" | custom-call | tf_op jit(solution)/shard_map/gather_weights/pallas_call | solution.py:175
  71.1 0.8 slice.129
  72.3 2.4 fusion.56
  75.7 0.8 pad_maximum_fusion.11
  76.4 3.0 %collective-permute-start.1 = (bf16[256,512]{1,0:T(8,128)(2,1)}, bf16[256,512]{1,0:T(8,128)(2,1)}, u32[]{:S(2)}, u32[]{:S(2)}) collective-permute-start(bf16[256,512]{1,0:T(8,128)(2,1)} %pad_maximum_fusion.11), channel_id=1, source_target_pairs={{0,8},{8,16},{16,24},{1,9},{9,17},{17,25},{2,10},{10,18},{18,26},{... | collective-permute-start | bytes 786440 | tf_op jit(solution)/shard_map/ppermute | solution.py:20
  79.4 3.4 %collective-permute-start = (bf16[256,512]{1,0:T(8,128)(2,1)}, bf16[256,512]{1,0:T(8,128)(2,1)}, u32[]{:S(2)}, u32[]{:S(2)}) collective-permute-start(bf16[256,512]{1,0:T(8,128)(2,1)} %pad_maximum_fusion.11), channel_id=1, source_target_pairs={{0,16},{8,24},{1,17},{9,25},{2,18},{10,26},{3,19},{11,27},{4,20},{... | collective-permute-start | bytes 786440 | tf_op jit(solution)/shard_map/ppermute | solution.py:20
  84.2 1.0 fusion.32
  85.6 3.5 %collective-permute-done = bf16[256,512]{1,0:T(8,128)(2,1)} collective-permute-done((bf16[256,512]{1,0:T(8,128)(2,1)}, bf16[256,512]{1,0:T(8,128)(2,1)}, u32[]{:S(2)}, u32[]{:S(2)}) %collective-permute-start) | collective-permute-done | bytes 262176 | tf_op jit(solution)/shard_map/ppermute | solution.py:20
  89.1 1.1 maximum_maximum_fusion
  91.4 0.7 fusion.18
  92.1 0.7 copy-done.9
  92.8 0.7 multiply_reduce_fusion.8
  94.4 1.9 fusion.93
  96.3 0.7 multiply_convert_fusion.1
  97.0 1.0 copy-done.35
  98.0 1.1 multiply_reduce_fusion.6
  99.4 1.0 fusion.44
  100.4 2.3 fusion.11
  102.8 2.5 %convolution_convert_fusion.1 = bf16[2048,640]{1,0:T(8,128)(2,1)} fusion(bf16[256,2048]{1,0:T(8,128)(2,1)S(1)} %multiply_convert_fusion.1, bf16[256,640]{1,0:T(8,128)(2,1)S(1)} %get-tuple-element.60), kind=kOutput, calls=%fused_computation.1 | convolution fusion | flops 672399360 | bytes 3997696 | tf_op jit(solution)/shard_map/dot_general | solution.py:45
  105.3 1.9 multiply_reduce_fusion.2
  108.6 0.7 copy-done.15
  109.4 1.4 convolution_convert_fusion.4
  110.8 2.0 copy.139
  112.8 2.6 %fusion.19 = f32[768,256]{1,0:T(8,128)} fusion(bf16[256,4,256]{0,2,1:T(8,128)(2,1)} %bitcast.154, f32[4,256,768]{1,2,0:T(8,128)S(1)} %get-tuple-element.83, f32[4,256]{1,0:T(4,128)S(1)} %log_add_fusion), kind=kOutput, calls=%fused_computation.40 | convolution fusion | flops 404226048 | bytes 4460544 | tf_op jit(solution)/shard_map/hqk,qhd->kd/dot_general | solution.py:533
  117.2 1.4 fusion.22
  118.6 0.7 fusion.16
  120.8 1.0 copy.115
  122.0 1.4 collective-permute-start.2
  123.5 1.5 collective-permute-start.3
  125.0 1.7 convolution_convert_fusion.3
  126.7 4.0 %convolution_convert_fusion = bf16[640,4096]{1,0:T(8,128)(2,1)} fusion(bf16[256,2048]{1,0:T(8,128)(2,1)S(1)} %copy-done.26, bf16[256,2048]{1,0:T(8,128)(2,1)S(1)} %copy-done.24, f32[256,640]{1,0:T(8,128)S(1)} %copy-done.3, f32[640]{0:T(1024)S(1)} %reshape.423, f32[256]{0:T(256)S(1)} %fusion.84), kind=kOutput, calls=%fused_computation | convolution fusion | flops 1349484544 | bytes 7998976 | tf_op jit(solution)/shard_map/dot_general | solution.py:45
  130.6 14.3 %collective-permute-done.3 = f32[256,512]{1,0:T(8,128)S(1)} collective-permute-done((f32[256,512]{1,0:T(8,128)S(1)}, f32[256,512]{1,0:T(8,128)S(1)}, u32[]{:S(2)}, u32[]{:S(2)}) %collective-permute-start.3) | collective-permute-done | bytes 524320 | tf_op jit(solution)/shard_map/ppermute | solution.py:20
  145.8 1.1 multiply_reduce_fusion.9
  146.9 1.1 fusion.65
  148.2 2.5 %fusion.39 = (f32[640]{0:T(1024)S(1)}, f32[256]{0:T(256)S(1)}, f32[256,640]{1,0:T(8,128)S(1)}) fusion(bf16[1,256,640]{2,1,0:T(8,128)(2,1)S(1)} %copy-done.8, f32[256]{0:T(256)S(1)} %fusion.81, f32[640]{0:T(1024)S(1)} %reshape.419, bf16[640,1536]{1,0:T(8,128)(2,1)} %bitcast.159, bf16[256,256]{0,1:T(8,128)(2,1)S(1)} %copy.123, ...), kind=kOutput, calls=%fused_computation.79 | convolution fusion | flops 506821760 | bytes 3742720 | tf_op jit(solution)/shard_map/dot_general | solution.py:51
  150.6 2.2 convolution_convert_fusion.2
  153.7 76.4 %reduce_grads.1 = (f32[80,1536]{1,0:T(8,128)}, f32[128,640]{1,0:T(8,128)}, f32[80,4096]{1,0:T(8,128)}, f32[256,640]{1,0:T(8,128)}, f32[8,384]{1,0:T(8,128)}) custom-call(bf16[8,80,1536]{2,1,0:T(8,128)(2,1)} %bitcast.160, bf16[8,128,640]{2,1,0:T(8,128)(2,1)} %bitcast.153, bf16[8,80,4096]{2,1,0:T(8,128)(2,1)} %bitcast.145, bf16[8,256,640]{2,1,0:T(8,128)(2,1)} %bitcast.146, ...), custom_call_target="tpu_custom_call" | custom-call | tf_op jit(solution)/shard_map/reduce_grads/pallas_call | solution.py:346
  230.2 1.3 slice_bitcast_fusion.6
  231.5 1.4 slice_bitcast_fusion.8
  232.9 1.6 fusion.96
  234.5 1.7 slice.151
  236.3 2.5 %fusion.95 = (f32[80,2048]{1,0:T(8,128)}, f32[80,2048]{1,0:T(8,128)}) fusion(f32[80,4096]{1,0:T(8,128)} %get-tuple-element.32), kind=kLoop, calls=%fused_computation.192 | loop fusion | bytes 2621440 | tf_op jit(solution)/shard_map/slice | solution.py:574
  238.8 0.9 fusion.54
  239.8 0.7 copy.149
  240.5 0.8 copy.150
  (140 shorter events, 12.3 us)
Async XLA Ops:
  0.6 71.4 %copy-start.8 = (bf16[1,256,640]{2,1,0:T(8,128)(2,1)S(1)}, bf16[1,256,640]{2,1,0:T(8,128)(2,1)}, u32[]{:S(2)}) copy-start(bf16[1,256,640]{2,1,0:T(8,128)(2,1)} %param.15) | copy-start | bytes 983044
  74.7 8.2 %copy-start.4 = (f32[256,1536]{1,0:T(8,128)}, f32[256,1536]{1,0:T(8,128)S(1)}, u32[]{:S(2)}) copy-start(f32[256,1536]{1,0:T(8,128)S(1)} %fusion.56) | copy-start | bytes 4718596
  75.7 9.7 %copy-start.19 = (f32[256,128]{1,0:T(8,128)}, f32[256,128]{1,0:T(8,128)S(1)}, u32[]{:S(2)}) copy-start(f32[256,128]{1,0:T(8,128)S(1)} %get-tuple-element.80) | copy-start | bytes 393220
  75.7 9.7 %copy-start.21 = (f32[256,128]{1,0:T(8,128)}, f32[256,128]{1,0:T(8,128)S(1)}, u32[]{:S(2)}) copy-start(f32[256,128]{1,0:T(8,128)S(1)} %get-tuple-element.81) | copy-start | bytes 393220
  76.4 9.1 %collective-permute-start.1 = (bf16[256,512]{1,0:T(8,128)(2,1)}, bf16[256,512]{1,0:T(8,128)(2,1)}, u32[]{:S(2)}, u32[]{:S(2)}) collective-permute-start(bf16[256,512]{1,0:T(8,128)(2,1)} %pad_maximum_fusion.11), channel_id=1, source_target_pairs={{0,8},{8,16},{16,24},{1,9},{9,17},{17,25},{2,10},{10,18},{18,26},{... | collective-permute-start | bytes 786440 | tf_op jit(solution)/shard_map/ppermute | solution.py:20
  79.4 9.7 %collective-permute-start = (bf16[256,512]{1,0:T(8,128)(2,1)}, bf16[256,512]{1,0:T(8,128)(2,1)}, u32[]{:S(2)}, u32[]{:S(2)}) collective-permute-start(bf16[256,512]{1,0:T(8,128)(2,1)} %pad_maximum_fusion.11), channel_id=1, source_target_pairs={{0,16},{8,24},{1,17},{9,25},{2,18},{10,26},{3,19},{11,27},{4,20},{... | collective-permute-start | bytes 786440 | tf_op jit(solution)/shard_map/ppermute | solution.py:20
  83.0 1.3 copy-start
  85.4 4.8 %copy-start.34 = (pred[256,768]{0,1:T(8,128)(4,1)S(1)}, pred[256,768]{0,1:T(8,128)(4,1)}, u32[]{:S(2)}) copy-start(pred[256,768]{0,1:T(8,128)(4,1)} %fusion.32) | copy-start | bytes 589828
  85.6 5.3 %copy-start.30 = (bf16[256,4,128]{2,0,1:T(8,128)(2,1)}, bf16[256,4,128]{2,0,1:T(8,128)(2,1)S(1)}, u32[]{:S(2)}) copy-start(bf16[256,4,128]{2,0,1:T(8,128)(2,1)S(1)} %get-tuple-element.58) | copy-start | bytes 786436
  85.6 5.3 %copy-start.32 = (bf16[256,4,128]{2,0,1:T(8,128)(2,1)}, bf16[256,4,128]{2,0,1:T(8,128)(2,1)S(1)}, u32[]{:S(2)}) copy-start(bf16[256,4,128]{2,0,1:T(8,128)(2,1)S(1)} %get-tuple-element.59) | copy-start | bytes 786436
  90.2 1.2 copy-start.11
  91.3 2.8 %slice-start = ((s8[5242880]{0:T(1024)(128)(4,1)}), s8[4194304]{0:T(1024)(128)(4,1)S(1)}, s32[]{:S(2)}) async-start(s8[5242880]{0:T(1024)(128)(4,1)} %bitcast.147), calls=%async_computation | async-start | bytes 8388608
  91.4 1.5 copy-start.9
  91.4 3.0 %slice-start.1 = ((s8[5242880]{0:T(1024)(128)(4,1)}), s8[1048576]{0:T(1024)(128)(4,1)S(1)}, s32[]{:S(2)}) async-start(s8[5242880]{0:T(1024)(128)(4,1)} %bitcast.147), calls=%async_computation.1 | async-start | bytes 2097152
  92.1 1.8 copy-start.17
  93.8 13.5 %copy-start.2 = (f32[256,640]{1,0:T(8,128)}, f32[256,640]{1,0:T(8,128)S(1)}, u32[]{:S(2)}) copy-start(f32[256,640]{1,0:T(8,128)S(1)} %get-tuple-element.49) | copy-start | bytes 1966084
  96.3 1.7 copy-start.35
  98.0 1.1 copy-start.14
  102.8 4.5 %copy-start.23 = (bf16[256,2048]{1,0:T(8,128)(2,1)}, bf16[256,2048]{1,0:T(8,128)(2,1)S(1)}, u32[]{:S(2)}) copy-start(bf16[256,2048]{1,0:T(8,128)(2,1)S(1)} %get-tuple-element.50) | copy-start | bytes 3145732
  102.8 4.5 %copy-start.25 = (bf16[256,2048]{1,0:T(8,128)(2,1)}, bf16[256,2048]{1,0:T(8,128)(2,1)S(1)}, u32[]{:S(2)}) copy-start(bf16[256,2048]{1,0:T(8,128)(2,1)S(1)} %get-tuple-element.51) | copy-start | bytes 3145732
  107.8 0.8 copy-start.6
  108.6 0.7 copy-start.15
  112.8 2.7 %copy-start.10 = (bf16[256,1024]{0,1:T(8,128)(2,1)S(1)}, bf16[256,1024]{0,1:T(8,128)(2,1)}, u32[]{:S(2)}) copy-start(bf16[256,1024]{0,1:T(8,128)(2,1)} %copy.139) | copy-start | bytes 1572868
  112.8 2.7 %copy-start.12 = (bf16[768,512]{1,0:T(8,128)(2,1)S(1)}, bf16[768,512]{1,0:T(8,128)(2,1)}, u32[]{:S(2)}) copy-start(bf16[768,512]{1,0:T(8,128)(2,1)} %copy-done.11) | copy-start | bytes 2359300
  116.1 1.0 copy-start.31
  116.1 1.0 copy-start.33
  118.6 1.0 copy-start.20
  118.6 1.0 copy-start.22
  118.6 1.4 copy-start.1
  120.4 1.5 copy-start.5
  120.4 1.5 copy-start.13
  120.8 4.2 %copy-start.16 = (bf16[256,640]{1,0:T(8,128)(2,1)S(1)}, bf16[256,640]{1,0:T(8,128)(2,1)}, u32[]{:S(2)}) copy-start(bf16[256,640]{1,0:T(8,128)(2,1)} %copy-done.15) | copy-start | bytes 983044
  120.8 4.2 %copy-start.18 = (bf16[256,4,256]{2,0,1:T(8,128)(2,1)S(1)}, bf16[256,4,256]{2,0,1:T(8,128)(2,1)}, u32[]{:S(2)}) copy-start(bf16[256,4,256]{2,0,1:T(8,128)(2,1)} %copy-done.17) | copy-start | bytes 1572868
  121.9 4.7 %copy-start.3 = (f32[256,640]{1,0:T(8,128)S(1)}, f32[256,640]{1,0:T(8,128)}, u32[]{:S(2)}) copy-start(f32[256,640]{1,0:T(8,128)} %copy-done.2) | copy-start | bytes 1966084
  121.9 4.7 %copy-start.24 = (bf16[256,2048]{1,0:T(8,128)(2,1)S(1)}, bf16[256,2048]{1,0:T(8,128)(2,1)}, u32[]{:S(2)}) copy-start(bf16[256,2048]{1,0:T(8,128)(2,1)} %copy-done.23) | copy-start | bytes 3145732
  121.9 4.7 %copy-start.26 = (bf16[256,2048]{1,0:T(8,128)(2,1)S(1)}, bf16[256,2048]{1,0:T(8,128)(2,1)}, u32[]{:S(2)}) copy-start(bf16[256,2048]{1,0:T(8,128)(2,1)} %copy-done.25) | copy-start | bytes 3145732
  122.0 8.6 %collective-permute-start.2 = (f32[256,512]{1,0:T(8,128)S(1)}, f32[256,512]{1,0:T(8,128)S(1)}, u32[]{:S(2)}, u32[]{:S(2)}) collective-permute-start(f32[256,512]{1,0:T(8,128)S(1)} %get-tuple-element.52), channel_id=1, source_target_pairs={{8,0},{16,8},{24,16},{9,1},{17,9},{25,17},{10,2},{18,10},{26,18},{... | collective-permute-start | bytes 1572872 | tf_op jit(solution)/shard_map/ppermute | solution.py:20
  123.5 21.5 %collective-permute-start.3 = (f32[256,512]{1,0:T(8,128)S(1)}, f32[256,512]{1,0:T(8,128)S(1)}, u32[]{:S(2)}, u32[]{:S(2)}) collective-permute-start(f32[256,512]{1,0:T(8,128)S(1)} %get-tuple-element.53), channel_id=1, source_target_pairs={{16,0},{24,8},{17,1},{25,9},{18,2},{26,10},{19,3},{27,11},{20,4},{... | collective-permute-start | bytes 1572872 | tf_op jit(solution)/shard_map/ppermute | solution.py:20
  130.6 17.5 %copy-start.28 = (bf16[256,4,256]{0,2,1:T(8,128)(2,1)S(1)}, bf16[256,4,256]{0,2,1:T(8,128)(2,1)}, u32[]{:S(2)}) copy-start(bf16[256,4,256]{0,2,1:T(8,128)(2,1)} %copy.115) | copy-start | bytes 1572868
  230.2 8.6 %copy-start.7 = (f32[256,640]{1,0:T(8,128)S(1)}, f32[256,640]{1,0:T(8,128)}, u32[]{:S(2)}) copy-start(f32[256,640]{1,0:T(8,128)} %copy-done.6) | copy-start | bytes 1966084
  236.3 3.5 %copy-start.29 = (f32[128,640]{1,0:T(8,128)S(1)}, f32[128,640]{1,0:T(8,128)}, u32[]{:S(2)}) copy-start(f32[128,640]{1,0:T(8,128)} %get-tuple-element.112) | copy-start | bytes 983044
  236.3 4.2 %copy-start.27 = (f32[256,640]{1,0:T(8,128)S(1)}, f32[256,640]{1,0:T(8,128)}, u32[]{:S(2)}) copy-start(f32[256,640]{1,0:T(8,128)} %get-tuple-element.115) | copy-start | bytes 1966084

commit v2 on v1

--- a/solution.py
+++ b/solution.py
@@ -66,18 +66,20 @@
     return jnp.where(lax.rem(owner, 2) == 0, owner // 2, size - 1 - owner // 2)
 
 
-def half_of(shape, by_rows, which):
+def region(shape, by_rows, core, plane=None):
+    size = shape[0 if by_rows else 1] // 2
+    start = core * size
+    if plane is not None:
+        size = size // 2
+        start = start + plane * size
+    if by_rows:
+        return (pl.ds(pl.multiple_of(start, size & -size), size), slice(None))
+    return (slice(None), pl.ds(pl.multiple_of(start, 128), size))
+
+
+def region_shape(shape, by_rows, cuts):
     rows, columns = shape
-    if by_rows:
-        size = rows // 2
-        return (pl.ds(pl.multiple_of(which * size, size & -size), size), slice(None))
-    size = columns // 2
-    return (slice(None), pl.ds(pl.multiple_of(which * size, 128), size))
-
-
-def half_shape(shape, by_rows):
-    rows, columns = shape
-    return (rows // 2, columns) if by_rows else (rows, columns // 2)
+    return (rows // cuts, columns) if by_rows else (rows, columns // cuts)
 
 
 def greet(peers):
@@ -87,58 +89,65 @@
     pl.semaphore_wait(barrier, len(peers))
 
 
-def gather_kernel(size, shapes, by_rows, *refs):
+def gather_kernel(size, shapes, by_rows, shared, places, *refs):
     count = len(shapes)
-    shards, gains = refs[:count], refs[count]
-    wholes, all_gains = refs[count + 1 : 2 * count + 1], refs[2 * count + 1]
-    own_sem, ring_send, ring_recv, pair_send, pair_recv = refs[2 * count + 2 :]
+    shards, gains = refs[: len(places)], refs[len(places)]
+    refs = refs[len(places) + 1 :]
+    wholes, all_gains = refs[:count], refs[count]
+    own_sem, ring_send, ring_recv, pair_send, pair_recv = refs[count + 1 : count + 6]
+    cross_send, cross_recv, relay_send, relay_recv = refs[count + 6 :]
     seq, me = lax.axis_index("seq"), lax.axis_index("fsdp")
-    core = lax.rem(seq, 2)
+    core, plane = lax.rem(seq, 2), lax.rem(seq // 2, 2)
     way = 1 - 2 * core
     place = ring_place(me, size)
     after = (seq, ring_owner(place + way, size))
     before = (seq, ring_owner(place - way, size))
     pair = (seq + way, me)
-    greet([after, before, pair])
-
-    def ring_copy(member, block, step, first=False):
+    across = (seq + 2 * (1 - 2 * plane), me)
+
+    own = []
+    for shard, (member, column) in zip(shards, places):
+        target = wholes[member].at[me, :, pl.ds(column, shard.shape[1])]
+        own.append(pltpu.make_async_copy(shard, target, own_sem.at[len(own)]))
+    own.append(pltpu.make_async_copy(gains, all_gains.at[me], own_sem.at[len(own)]))
+    for copy in own:
+        copy.start()
+    greet([after, before, pair, across])
+
+    def copy_of(member, block, core, plane, sems, step, device):
         if member == count:
-            source, target = gains if first else all_gains.at[block], all_gains.at[block]
+            target = all_gains.at[block]
         else:
-            part = half_of(shapes[member], by_rows[member], core)
+            part = region(shapes[member], by_rows[member], core, plane)
             target = wholes[member].at[(block, *part)]
-            source = shards[member].at[part] if first else target
-        return pltpu.make_async_remote_copy(
-            src_ref=source,
-            dst_ref=target,
-            send_sem=ring_send.at[step, member],
-            recv_sem=ring_recv.at[step, member],
-            device_id=after,
-            device_id_type=MESH,
-        )
-
-    def pair_copy(member, block, step, which):
-        part = half_of(shapes[member], by_rows[member], which)
-        target = wholes[member].at[(block, *part)]
         return pltpu.make_async_remote_copy(
             src_ref=target,
             dst_ref=target,
-            send_sem=pair_send.at[step, member],
-            recv_sem=pair_recv.at[step, member],
-            device_id=pair,
+            send_sem=sems[0].at[step, member],
+            recv_sem=sems[1].at[step, member],
+            device_id=device,
             device_id_type=MESH,
         )
 
-    own = []
+    def plane_of(member):
+        return plane if member < count and shared[member] else None
+
+    def ring_copy(member, block, step):
+        return copy_of(member, block, core, plane_of(member), (ring_send, ring_recv), step, after)
+
+    def pair_copy(member, block, step, core):
+        return copy_of(member, block, core, plane_of(member), (pair_send, pair_recv), step, pair)
+
+    def cross_copy(member, block, step, plane):
+        return copy_of(member, block, core, plane, (cross_send, cross_recv), step, across)
+
+    def relay_copy(member, block, step, core):
+        return copy_of(member, block, core, 1 - plane, (relay_send, relay_recv), step, pair)
+
+    for copy in own:
+        copy.wait()
     for member in range(count + 1):
-        ring_copy(member, me, 0, first=True).start()
-    for member in range(count):
-        own.append(
-            pltpu.make_async_copy(shards[member], wholes[member].at[me], own_sem.at[member])
-        )
-    own.append(pltpu.make_async_copy(gains, all_gains.at[me], own_sem.at[count]))
-    for copy in own:
-        copy.start()
+        ring_copy(member, me, 0).start()
 
     def arrive(step, forward):
         block = ring_owner(place - way * step, size)
@@ -147,45 +156,71 @@
             if forward:
                 ring_copy(member, block, step).start()
             if member < count:
+                if shared[member]:
+                    cross_copy(member, block, step - 1, plane).start()
                 pair_copy(member, block, step - 1, core).start()
 
-    lax.fori_loop(1, size - 1, lambda step, _: (arrive(step, True), 0)[1], 0)
+    def relay(step):
+        block = ring_owner(place - way * step, size)
+        for member in range(count):
+            if shared[member]:
+                cross_copy(member, block, step - 1, 1 - plane).wait_recv()
+                relay_copy(member, block, step - 1, core).start()
+
+    arrive(1, True)
+
+    def turn(step, _):
+        arrive(step, True)
+        relay(step - 1)
+        return 0
+
+    lax.fori_loop(2, size - 1, turn, 0)
     arrive(size - 1, False)
-    for copy in own:
-        copy.wait()
+    relay(size - 2)
+    relay(size - 1)
 
     def finish(step, _):
+        block = ring_owner(place + way * (step + 1), size)
         for member in range(count + 1):
             ring_copy(member, me, step).wait_send()
             if member < count:
                 pair_copy(member, me, step, core).wait_send()
-                block = ring_owner(place + way * (step + 1), size)
                 pair_copy(member, block, step, 1 - core).wait_recv()
+                if shared[member]:
+                    cross_copy(member, me, step, plane).wait_send()
+                    relay_copy(member, me, step, core).wait_send()
+                    relay_copy(member, block, step, 1 - core).wait_recv()
         return 0
 
     lax.fori_loop(0, size - 1, finish, 0)
 
 
-def gather_weights(shards, by_rows, gains):
+def gather_weights(shards, groups, by_rows, shared, gains):
     size = lax.axis_size("fsdp")
-    shapes = [shard.shape for shard in shards]
-    count = len(shards)
+    shapes, places = [], []
+    for number, group in enumerate(groups):
+        column = 0
+        for member in group:
+            places.append((number, column))
+            column += shards[member].shape[1]
+        shapes.append((shards[group[0]].shape[0], column))
+    count = len(groups)
     any_space = pl.BlockSpec(memory_space=pl.ANY)
     copies = pltpu.SemaphoreType.DMA((size - 1, count + 1))
     return pl.pallas_call(
-        functools.partial(gather_kernel, size, shapes, by_rows),
+        functools.partial(gather_kernel, size, shapes, by_rows, shared, places),
         out_shape=[
-            jax.ShapeDtypeStruct((size, *member.shape), member.dtype) for member in (*shards, gains)
+            jax.ShapeDtypeStruct((size, *shape), gains.dtype) for shape in (*shapes, gains.shape)
         ],
-        in_specs=[any_space] * (count + 1),
+        in_specs=[any_space] * (len(shards) + 1),
         out_specs=[any_space] * (count + 1),
-        scratch_shapes=[pltpu.SemaphoreType.DMA((count + 1,)), copies, copies, copies, copies],
+        scratch_shapes=[pltpu.SemaphoreType.DMA((len(shards) + 1,)), *[copies] * 8],
         compiler_params=pltpu.CompilerParams(collective_id=0, has_side_effects=True),
         name="gather_weights",
     )(*shards, gains)
 
 
-def reduce_kernel(size, blocks, shapes, by_rows, *refs):
+def reduce_kernel(size, blocks, shapes, by_rows, shared, places, *refs):
     count = len(shapes)
     every = list(refs)
 
@@ -195,51 +230,71 @@
         return taken
 
     mine, (gain_mine,) = take(count), take(1)
-    totals, (gain_total,) = take(count), take(1)
-    parts, landed, spread = take(count), take(count), take(count)
+    results, (gain_total,) = take(len(places)), take(1)
+    totals, parts, landed, crossed = take(count), take(count), take(count), take(count)
+    spread, agreed = take(count), take(count)
     gain_sent, gain_landed, gain_spread = take(3)
-    pair_send, pair_recv, ring_send, ring_recv = take(4)
-    spread_send, spread_recv, gain_send, gain_recv, last_send, last_recv = take(6)
+    pair_send, pair_recv, ring_send, ring_recv, cross_send, cross_recv = take(6)
+    spread_send, spread_recv, gain_send, gain_recv = take(4)
+    agree_send, agree_recv, last_send, last_recv = take(4)
 
     seq, me = lax.axis_index("seq"), lax.axis_index("fsdp")
-    core = lax.rem(seq, 2)
-    row = seq // 2
-    rows = blocks // 2
+    core, plane = lax.rem(seq, 2), lax.rem(seq // 2, 2)
     way = 1 - 2 * core
     place = ring_place(me, size)
     after = (seq, ring_owner(place + way, size))
     before = (seq, ring_owner(place - way, size))
     pair = (seq + way, me)
+    across = (seq + 2 * (1 - 2 * plane), me)
     others = [(lax.rem(seq + by, blocks), me) for by in range(1, blocks)]
     greet([after, before, *others])
 
-    def remote(source, target, send_sem, recv_sem, device):
+    def remote(source, target, sems, index, device):
         return pltpu.make_async_remote_copy(
             src_ref=source,
             dst_ref=target,
-            send_sem=send_sem,
-            recv_sem=recv_sem,
+            send_sem=sems[0].at[index],
+            recv_sem=sems[1].at[index],
             device_id=device,
             device_id_type=MESH,
         )
 
+    def block_at(step):
+        return ring_owner(place - way * (1 + step), size)
+
+    def within(member, part):
+        shape = region_shape(shapes[member], by_rows[member], 2)
+        return region(shape, by_rows[member], part)
+
+    def ring_part(member):
+        return within(member, plane) if shared[member] else (slice(None), slice(None))
+
+    def own_part(member, part):
+        return region(shapes[member], by_rows[member], core, part if shared[member] else None)
+
     def pair_copy(member, step):
         block = ring_owner(place + way * (1 + step), size)
-        part = half_of(shapes[member], by_rows[member], 1 - core)
+        part = region(shapes[member], by_rows[member], 1 - core)
         return remote(
             mine[member].at[(block, *part)],
             parts[member].at[block],
-            pair_send.at[step, member],
-            pair_recv.at[step, member],
+            (pair_send, pair_recv),
+            (step, member),
             pair,
         )
 
     def ring_copy(member, step):
-        block = ring_owner(place - way * (1 + step), size)
-        source = gain_sent.at[step] if member == count else parts[member].at[block]
-        target = gain_landed.at[step] if member == count else landed[member].at[step]
+        if member == count:
+            source, target = gain_sent.at[step], gain_landed.at[step]
+        else:
+            source = parts[member].at[(block_at(step), *ring_part(member))]
+            target = landed[member].at[step]
+        return remote(source, target, (ring_send, ring_recv), (step, member), after)
+
+    def cross_copy(member, step):
+        source = parts[member].at[(block_at(step), *within(member, 1 - plane))]
         return remote(
-            source, target, ring_send.at[step, member], ring_recv.at[step, member], after
+            source, crossed[member].at[step], (cross_send, cross_recv), (step, member), across
         )
 
     def start_pair(step, _):
@@ -249,22 +304,35 @@
 
     lax.fori_loop(0, size, start_pair, 0)
 
-    def add_up(step, first, last):
-        block = ring_owner(place - way * (1 + step), size)
+    def prepare(step):
+        block = block_at(step)
         for member in range(count):
             pair_copy(member, step).wait_recv()
-            part = half_of(shapes[member], by_rows[member], core)
-            total = mine[member][(block, *part)].astype(jnp.float32)
-            total = total + parts[member][block].astype(jnp.float32)
+            if shared[member]:
+                spot = (block, *within(member, 1 - plane))
+                total = mine[member][(block, *own_part(member, 1 - plane))].astype(jnp.float32)
+                total = total + parts[member][spot].astype(jnp.float32)
+                parts[member][spot] = total.astype(jnp.bfloat16)
+                cross_copy(member, step).start()
+
+    def add_up(step, first, last):
+        block = block_at(step)
+        for member in range(count):
+            spot = (block, *ring_part(member))
+            total = mine[member][(block, *own_part(member, plane))].astype(jnp.float32)
+            total = total + parts[member][spot].astype(jnp.float32)
+            if shared[member]:
+                cross_copy(member, step).wait_recv()
+                total = total + crossed[member][step].astype(jnp.float32)
             if not first:
                 ring_copy(member, step - 1).wait_recv()
                 total = total + landed[member][step - 1].astype(jnp.float32)
             if last:
-                spread[member][row] = total.astype(jnp.bfloat16)
-                for by in range(1, rows):
+                spread[member][row_of(member)] = total.astype(jnp.bfloat16)
+                for by in range(1, rows_of(member)):
                     spread_copy(member, by).start()
             else:
-                parts[member][block] = total.astype(jnp.bfloat16)
+                parts[member][spot] = total.astype(jnp.bfloat16)
                 ring_copy(member, step).start()
         total = gain_mine[block]
         if not first:
@@ -278,34 +346,62 @@
             gain_sent[step] = total
             ring_copy(count, step).start()
 
+    def stride_of(member):
+        return 4 if shared[member] else 2
+
+    def row_of(member):
+        return seq // stride_of(member)
+
+    def rows_of(member):
+        return blocks // stride_of(member)
+
     def spread_copy(member, by):
-        target = spread[member].at[row]
-        device = (lax.rem(seq + 2 * by, blocks), me)
-        return remote(
-            target, target, spread_send.at[by - 1, member], spread_recv.at[by - 1, member], device
-        )
+        target = spread[member].at[row_of(member)]
+        device = (lax.rem(seq + stride_of(member) * by, blocks), me)
+        return remote(target, target, (spread_send, spread_recv), (by - 1, member), device)
 
     def gain_copy(by):
         target = gain_spread.at[seq]
-        return remote(
-            target, target, gain_send.at[by - 1], gain_recv.at[by - 1], others[by - 1]
-        )
+        return remote(target, target, (gain_send, gain_recv), by - 1, others[by - 1])
+
+    def agree_copy(member):
+        target = agreed[member].at[within(member, plane)]
+        return remote(target, target, (agree_send, agree_recv), member, across)
 
     def last_copy(member):
-        target = totals[member].at[half_of(shapes[member], by_rows[member], core)]
-        return remote(target, target, last_send.at[member], last_recv.at[member], pair)
-
+        target = totals[member].at[region(shapes[member], by_rows[member], core)]
+        return remote(target, target, (last_send, last_recv), member, pair)
+
+    prepare(0)
+    prepare(1)
     add_up(0, True, False)
-    lax.fori_loop(1, size - 1, lambda step, _: (add_up(step, False, False), 0)[1], 0)
+
+    def turn(step, _):
+        prepare(step + 1)
+        add_up(step, False, False)
+        return 0
+
+    lax.fori_loop(1, size - 1, turn, 0)
     add_up(size - 1, False, True)
-    for member in range(count):
-        for by in range(1, rows):
+    order = sorted(range(count), key=lambda member: not shared[member])
+    for member in order:
+        for by in range(1, rows_of(member)):
             spread_copy(member, by).wait_recv()
         total = spread[member][0].astype(jnp.float32)
-        for other in range(1, rows):
+        for other in range(1, rows_of(member)):
             total = total + spread[member][other].astype(jnp.float32)
-        totals[member][half_of(shapes[member], by_rows[member], core)] = total
-        last_copy(member).start()
+        if shared[member]:
+            agreed[member][within(member, plane)] = total.astype(jnp.bfloat16)
+            agree_copy(member).start()
+        else:
+            totals[member][region(shapes[member], by_rows[member], core)] = total
+            last_copy(member).start()
+    for member in order:
+        if shared[member]:
+            agree_copy(member).wait_recv()
+            total = agreed[member][...].astype(jnp.float32)
+            totals[member][region(shapes[member], by_rows[member], core)] = total
+            last_copy(member).start()
     for by in range(1, blocks):
         gain_copy(by).wait_recv()
     total = gain_spread[0]
@@ -323,35 +419,62 @@
     def finish_pair(step, _):
         for member in range(count):
             pair_copy(member, step).wait_send()
+            if shared[member]:
+                cross_copy(member, step).wait_send()
         return 0
 
     lax.fori_loop(0, size, finish_pair, 0)
     for member in range(count):
-        for by in range(1, rows):
+        for by in range(1, rows_of(member)):
             spread_copy(member, by).wait_send()
+        if shared[member]:
+            agree_copy(member).wait_send()
         last_copy(member).wait()
     for by in range(1, blocks):
         gain_copy(by).wait_send()
-
-
-def reduce_grads(grads, by_rows, gain_grads):
+    for result, (member, column) in zip(results, places):
+        result[...] = totals[member][:, column : column + result.shape[1]]
+
+
+def reduce_grads(grads, widths, by_rows, shared, gain_grads):
     size, blocks = lax.axis_size("fsdp"), lax.axis_size("seq")
     shapes = [grad.shape[1:] for grad in grads]
-    halves = [half_shape(*both) for both in zip(shapes, by_rows)]
     count = len(grads)
+    halves = [region_shape(shapes[m], by_rows[m], 2) for m in range(count)]
+    pieces = [region_shape(shapes[m], by_rows[m], 4 if shared[m] else 2) for m in range(count)]
+    places, results = [], []
+    for member in range(count):
+        column = 0
+        for width in widths[member]:
+            places.append((member, column))
+            results.append((shapes[member][0], width))
+            column += width
     gain_shape = gain_grads.shape[1:]
-    rows = blocks // 2
     in_vmem = pl.BlockSpec(memory_space=pltpu.VMEM)
     dma = pltpu.SemaphoreType.DMA
+    unused = (16, 128)
+
+    def buffers(lengths, extents):
+        return [
+            pltpu.VMEM((*length, *extent), jnp.bfloat16)
+            for length, extent in zip(lengths, extents)
+        ]
+
     return pl.pallas_call(
-        functools.partial(reduce_kernel, size, blocks, shapes, by_rows),
-        out_shape=[jax.ShapeDtypeStruct(shape, jnp.float32) for shape in (*shapes, gain_shape)],
+        functools.partial(reduce_kernel, size, blocks, shapes, by_rows, shared, places),
+        out_shape=[jax.ShapeDtypeStruct(shape, jnp.float32) for shape in (*results, gain_shape)],
         in_specs=[in_vmem] * (count + 1),
-        out_specs=[in_vmem] * (count + 1),
+        out_specs=[in_vmem] * (len(results) + 1),
         scratch_shapes=[
-            *[pltpu.VMEM((size, *half), jnp.bfloat16) for half in halves],
-            *[pltpu.VMEM((size - 1, *half), jnp.bfloat16) for half in halves],
-            *[pltpu.VMEM((rows, *half), jnp.bfloat16) for half in halves],
+            *[pltpu.VMEM(shape, jnp.float32) for shape in shapes],
+            *buffers([(size,)] * count, halves),
+            *buffers([(size - 1,)] * count, pieces),
+            *buffers(
+                [(size,) if member else () for member in shared],
+                [pieces[m] if shared[m] else unused for m in range(count)],
+            ),
+            *buffers([(blocks // (4 if member else 2),) for member in shared], pieces),
+            *buffers([()] * count, [halves[m] if shared[m] else unused for m in range(count)]),
             pltpu.VMEM((size - 1, *gain_shape), jnp.float32),
             pltpu.VMEM((size - 1, *gain_shape), jnp.float32),
             pltpu.VMEM((blocks, *gain_shape), jnp.float32),
@@ -359,10 +482,14 @@
             dma((size, count)),
             dma((size - 1, count + 1)),
             dma((size - 1, count + 1)),
-            dma((rows, count)),
-            dma((rows, count)),
+            dma((size, count)),
+            dma((size, count)),
+            dma((blocks // 2, count)),
+            dma((blocks // 2, count)),
             dma((blocks,)),
             dma((blocks,)),
+            dma((count,)),
+            dma((count,)),
             dma((count,)),
             dma((count,)),
         ],
@@ -406,16 +533,15 @@
     key_norm,
 ):
     size = lax.axis_size("fsdp")
-    shards = (
-        jnp.concatenate([query_proj, key_proj, value_proj], axis=1),
-        output_proj,
-        jnp.concatenate([gate_proj, up_proj], axis=1),
-        down_proj,
-    )
+    shards = (query_proj, key_proj, value_proj, output_proj, gate_proj, up_proj, down_proj)
+    groups = ((0, 1, 2), (3,), (4, 5), (6,))
     by_rows = (False, True, False, True)
+    shared = (False, True, True, False)
     gain_shards = (attn_norm, attn_post_norm, ffn_norm, ffn_post_norm, query_norm, key_norm)
     widths = [member.shape[0] for member in gain_shards]
-    *wholes, all_gains = gather_weights(shards, by_rows, pack_gains(gain_shards, 16, ()))
+    *wholes, all_gains = gather_weights(
+        shards, groups, by_rows, shared, pack_gains(gain_shards, 16, ())
+    )
     into_w, output_w, ffn_w, down_w = (whole.reshape(-1, whole.shape[-1]) for whole in wholes)
     query_width, head_width = query_proj.shape[1], key_proj.shape[1]
     ffn_width = gate_proj.shape[1]
@@ -560,19 +686,12 @@
     gain_grads = pack_gains(
         (grad_pre1, grad_post1, grad_pre2, grad_post2, grad_qgain, grad_kgain), 8, (size,)
     )
-    into_total, output_total, ffn_total, down_total, gain_total = reduce_grads(
-        grads, by_rows, gain_grads
-    )
+    piece_widths = [[shards[member].shape[1] for member in group] for group in groups]
+    *results, gain_total = reduce_grads(grads, piece_widths, by_rows, shared, gain_grads)
     return (
         result.astype(jnp.bfloat16)[None],
         grad_input.astype(jnp.bfloat16)[None],
-        into_total[:, :query_width],
-        into_total[:, query_width : query_width + head_width],
-        into_total[:, query_width + head_width :],
-        output_total,
-        ffn_total[:, :ffn_width],
-        ffn_total[:, ffn_width:],
-        down_total,
+        *results,
         *unpack_gains(gain_total[0], widths),
     )
 

time: 242 us -> 258 us (1.066)
  Pallas kernels: 138 us -> 161 us
  other arithmetic: 17.3 us -> 13.8 us
    pallas_call x1, Pallas kernels: 62.1 us -> 93.9 us  [gather_weights(): pl.pallas_call(functools.partial(gather_kernel, size, shapes, by_rows, sh...]
    pallas_call x1, Pallas kernels: 76.4 us -> 67.3 us  [reduce_grads(): pl.pallas_call(functools.partial(reduce_kernel, size, blocks, shapes, by_...]
    slice x3 -> x0, local copies, waits for them, and re-layouts: 5.86 us -> none  [the longest x1 2.55 us: on_device(): ffn_total[:, ffn_width:]]
    unnamed x79 -> x94, local copies, waits for them, and re-layouts: 5.97 us -> 9.76 us
    concatenate x2 -> x0, other arithmetic: 3.67 us -> none  [the longest x1 1.99 us: on_device(): jnp.concatenate([gate_proj, up_proj], axis=1)]
where the time goes in v2:
time: 258 us; the launch traced here: 257 us
  Pallas kernels  161 us (62%)
  matrix products  31.5 us (12%)
  local copies, waits for them, and re-layouts  23.6 us (9%)
  waiting for transfers between devices  17.6 us (7%)
  other arithmetic  13.8 us (5%)
  starting transfers between devices  8.34 us (3%)
    pallas_call x1, Pallas kernels, gather_weights(): pl.pallas_call(functools.partial(gather_kernel, size, shapes, by_rows, sh...  93.9 us
    pallas_call x1, Pallas kernels, reduce_grads(): pl.pallas_call(functools.partial(reduce_kernel, size, blocks, shapes, by_...  67.3 us
    ppermute x4, waiting for transfers between devices, shifted(): return lax.ppermute(array, axis, pairs)  17.6 us
    dot_general x4, matrix products, row_outer(): lax.dot_general(left, right, (((0,), (0,)), ((), ())), preferred_element_...  10.3 us
    unnamed x94, local copies, waits for them, and re-layouts  9.76 us
    ppermute x4, starting transfers between devices, shifted(): return lax.ppermute(array, axis, pairs)  8.34 us
    dot_general x4, matrix products, back_product(): lax.dot_general(grad_rows, weight, (((1,), (1,)), ((), ())), preferred_el...  8.18 us
  transfers between devices with their start and end apart: 4, of which 2 were waited for; matrix products, arithmetic and copies ran while one was open for 3% of the time, Pallas kernels for 0%

profile of v2, /device:TPU:0, one launch (start us, length us, event | category | flops | bytes accessed | tf_op | source)
XLA Modules:
  0.0 257.5 jit_solution(14170527288699562331)
XLA Ops:
  0.7 4.1 %concatenate.28 = bf16[384]{0:T(512)(128)(2,1)S(1)} concatenate(bf16[80]{0:T(256)(128)(2,1)} %param.24, bf16[80]{0:T(256)(128)(2,1)} %param.25, bf16[80]{0:T(256)(128)(2,1)} %param.26, bf16[80]{0:T(256)(128)(2,1)} %param.27, bf16[32]{0:T(256)(128)(2,1)} %param.28, bf16[32]{0:T(256)(128)(2,1)} %param.29), dimensions={0} | concatenate | bytes 1536 | tf_op jit(solution)/shard_map/concatenate | solution.py:504
  5.4 93.9 %gather_weights.1 = (bf16[8,80,1536]{2,1,0:T(8,128)(2,1)}, bf16[8,128,640]{2,1,0:T(8,128)(2,1)}, bf16[8,80,4096]{2,1,0:T(8,128)(2,1)}, bf16[8,256,640]{2,1,0:T(8,128)(2,1)}, bf16[8,16,384]{2,1,0:T(8,128)(2,1)}) custom-call(bf16[80,1024]{1,0:T(8,128)(2,1)} %refs_0_.1, bf16[80,256]{1,0:T(8,128)(2,1)} %refs_1_.1, bf16[80,256]{1,0:T(8,128)(2,1)} %refs_2_.1, ...), custom_call_target="tpu_custom_call" | custom-call | tf_op jit(solution)/shard_map/gather_weights/pallas_call | solution.py:210
  99.3 0.8 slice.114
  100.2 1.1 fusion.40
  101.4 2.5 fusion.56
  104.9 3.0 %collective-permute-start.1 = (bf16[256,512]{1,0:T(8,128)(2,1)S(1)}, bf16[256,512]{1,0:T(8,128)(2,1)}, u32[]{:S(2)}, u32[]{:S(2)}) collective-permute-start(bf16[256,512]{1,0:T(8,128)(2,1)S(1)} %pad_maximum_fusion.10), channel_id=1, source_target_pairs={{0,8},{8,16},{16,24},{1,9},{9,17},{17,25},{2,10},{10,18},{18,26},{... | collective-permute-start | bytes 786440 | tf_op jit(solution)/shard_map/ppermute | solution.py:20
  107.9 2.4 collective-permute-start
  111.7 1.0 fusion.32
  113.1 3.2 %collective-permute-done = bf16[256,512]{1,0:T(8,128)(2,1)} collective-permute-done((bf16[256,512]{1,0:T(8,128)(2,1)S(1)}, bf16[256,512]{1,0:T(8,128)(2,1)}, u32[]{:S(2)}, u32[]{:S(2)}) %collective-permute-start) | collective-permute-done | bytes 262176 | tf_op jit(solution)/shard_map/ppermute | solution.py:20
  116.3 1.1 maximum_maximum_fusion
  117.4 0.7 fusion.95
  118.6 0.7 fusion.18
  119.3 0.7 copy-done.9
  120.0 0.7 multiply_reduce_fusion.8
  121.7 1.9 fusion.93
  123.6 0.7 multiply_convert_fusion.1
  124.3 1.0 copy-done.40
  125.3 1.1 multiply_reduce_fusion.6
  126.7 1.0 fusion.44
  127.7 2.3 fusion.11
  130.1 2.5 convolution_convert_fusion.1
  132.6 1.9 multiply_reduce_fusion.2
  135.9 0.7 copy-done.15
  136.6 1.4 convolution_convert_fusion.4
  138.0 2.1 copy.139
  140.1 2.6 %fusion.19 = f32[768,256]{1,0:T(8,128)} fusion(bf16[256,4,256]{0,2,1:T(8,128)(2,1)} %bitcast.154, f32[4,256,768]{1,2,0:T(8,128)S(1)} %get-tuple-element.85, f32[4,256]{1,0:T(4,128)S(1)} %log_add_fusion), kind=kOutput, calls=%fused_computation.40 | convolution fusion | flops 404226048 | bytes 4460544 | tf_op jit(solution)/shard_map/hqk,qhd->kd/dot_general | solution.py:659
  142.7 0.7 fusion
  144.4 1.5 fusion.22
  145.9 0.7 fusion.16
  148.1 1.0 copy.115
  149.3 1.4 collective-permute-start.2
  150.8 1.5 collective-permute-start.3
  152.3 1.7 convolution_convert_fusion.3
  154.0 3.9 %convolution_convert_fusion = bf16[640,4096]{1,0:T(8,128)(2,1)} fusion(bf16[256,2048]{1,0:T(8,128)(2,1)S(1)} %copy-done.26, bf16[256,2048]{1,0:T(8,128)(2,1)S(1)} %copy-done.24, f32[256,640]{1,0:T(8,128)S(1)} %copy-done.3, f32[640]{0:T(1024)S(1)} %reshape.423, f32[256]{0:T(256)S(1)} %fusion.84), kind=kOutput, calls=%fused_computation | convolution fusion | flops 1349484544 | bytes 7998976 | tf_op jit(solution)/shard_map/dot_general | solution.py:45
  157.9 14.4 %collective-permute-done.3 = f32[256,512]{1,0:T(8,128)S(1)} collective-permute-done((f32[256,512]{1,0:T(8,128)S(1)}, f32[256,512]{1,0:T(8,128)S(1)}, u32[]{:S(2)}, u32[]{:S(2)}) %collective-permute-start.3) | collective-permute-done | bytes 524320 | tf_op jit(solution)/shard_map/ppermute | solution.py:20
  173.2 1.1 multiply_reduce_fusion.9
  174.3 1.1 fusion.65
  175.5 2.5 fusion.39
  178.0 2.2 convolution_convert_fusion.2
  181.1 67.3 %reduce_grads.1 = (f32[80,1024]{1,0:T(8,128)}, f32[80,256]{1,0:T(8,128)}, f32[80,256]{1,0:T(8,128)}, f32[128,640]{1,0:T(8,128)}, f32[80,2048]{1,0:T(8,128)}, /*i...) custom-call(bf16[8,80,1536]{2,1,0:T(8,128)(2,1)} %bitcast.160, bf16[8,128,640]{2,1,0:T(8,128)(2,1)} %bitcast.153, ...), custom_call_target="tpu_custom_call" | custom-call | tf_op jit(solution)/shard_map/reduce_grads/pallas_call | solution.py:463
  248.5 1.4 slice_bitcast_fusion.6
  249.8 1.4 slice_bitcast_fusion.8
  251.3 0.9 fusion.54
  252.2 0.7 copy.154
  254.2 0.7 copy.157
  255.0 0.8 copy.158
  255.8 0.8 copy.159
  256.6 0.8 copy.160
  (150 shorter events, 12.3 us)
Async XLA Ops:
  103.9 6.5 %copy-start.4 = (f32[256,1536]{1,0:T(8,128)}, f32[256,1536]{1,0:T(8,128)S(1)}, u32[]{:S(2)}) copy-start(f32[256,1536]{1,0:T(8,128)S(1)} %fusion.56) | copy-start | bytes 4718596
  104.9 8.0 %copy-start.19 = (f32[256,128]{1,0:T(8,128)}, f32[256,128]{1,0:T(8,128)S(1)}, u32[]{:S(2)}) copy-start(f32[256,128]{1,0:T(8,128)S(1)} %get-tuple-element.82) | copy-start | bytes 393220
  104.9 8.0 %copy-start.21 = (f32[256,128]{1,0:T(8,128)}, f32[256,128]{1,0:T(8,128)S(1)}, u32[]{:S(2)}) copy-start(f32[256,128]{1,0:T(8,128)S(1)} %get-tuple-element.83) | copy-start | bytes 393220
  104.9 8.2 %collective-permute-start.1 = (bf16[256,512]{1,0:T(8,128)(2,1)S(1)}, bf16[256,512]{1,0:T(8,128)(2,1)}, u32[]{:S(2)}, u32[]{:S(2)}) collective-permute-start(bf16[256,512]{1,0:T(8,128)(2,1)S(1)} %pad_maximum_fusion.10), channel_id=1, source_target_pairs={{0,8},{8,16},{16,24},{1,9},{9,17},{17,25},{2,10},{10,18},{18,26},{... | collective-permute-start | bytes 786440 | tf_op jit(solution)/shard_map/ppermute | solution.py:20
  107.9 8.4 %collective-permute-start = (bf16[256,512]{1,0:T(8,128)(2,1)S(1)}, bf16[256,512]{1,0:T(8,128)(2,1)}, u32[]{:S(2)}, u32[]{:S(2)}) collective-permute-start(bf16[256,512]{1,0:T(8,128)(2,1)S(1)} %pad_maximum_fusion.10), channel_id=1, source_target_pairs={{0,16},{8,24},{1,17},{9,25},{2,18},{10,26},{3,19},{11,27},{4,20},{... | collective-permute-start | bytes 786440 | tf_op jit(solution)/shard_map/ppermute | solution.py:20
  110.4 1.3 copy-start
  112.9 4.5 %copy-start.37 = (pred[256,768]{0,1:T(8,128)(4,1)S(1)}, pred[256,768]{0,1:T(8,128)(4,1)}, u32[]{:S(2)}) copy-start(pred[256,768]{0,1:T(8,128)(4,1)} %fusion.32) | copy-start | bytes 589828
  113.1 5.0 %copy-start.33 = (bf16[256,4,128]{2,0,1:T(8,128)(2,1)}, bf16[256,4,128]{2,0,1:T(8,128)(2,1)S(1)}, u32[]{:S(2)}) copy-start(bf16[256,4,128]{2,0,1:T(8,128)(2,1)S(1)} %get-tuple-element.62) | copy-start | bytes 786436
  113.1 5.0 %copy-start.35 = (bf16[256,4,128]{2,0,1:T(8,128)(2,1)}, bf16[256,4,128]{2,0,1:T(8,128)(2,1)S(1)}, u32[]{:S(2)}) copy-start(bf16[256,4,128]{2,0,1:T(8,128)(2,1)S(1)} %get-tuple-element.63) | copy-start | bytes 786436
  117.4 1.2 copy-start.11
  118.5 2.9 %slice-start = ((s8[5242880]{0:T(1024)(128)(4,1)}), s8[4194304]{0:T(1024)(128)(4,1)S(1)}, s32[]{:S(2)}) async-start(s8[5242880]{0:T(1024)(128)(4,1)} %bitcast.147), calls=%async_computation | async-start | bytes 8388608
  118.5 1.5 copy-start.9
  118.5 3.1 %slice-start.1 = ((s8[5242880]{0:T(1024)(128)(4,1)}), s8[1048576]{0:T(1024)(128)(4,1)S(1)}, s32[]{:S(2)}) async-start(s8[5242880]{0:T(1024)(128)(4,1)} %bitcast.147), calls=%async_computation.1 | async-start | bytes 2097152
  119.3 2.0 copy-start.17
  119.3 1.6 copy-start.8
  121.2 13.4 %copy-start.2 = (f32[256,640]{1,0:T(8,128)}, f32[256,640]{1,0:T(8,128)S(1)}, u32[]{:S(2)}) copy-start(f32[256,640]{1,0:T(8,128)S(1)} %get-tuple-element.55) | copy-start | bytes 1966084
  123.5 1.7 copy-start.40
  125.3 1.1 copy-start.14
  130.1 4.5 %copy-start.23 = (bf16[256,2048]{1,0:T(8,128)(2,1)}, bf16[256,2048]{1,0:T(8,128)(2,1)S(1)}, u32[]{:S(2)}) copy-start(bf16[256,2048]{1,0:T(8,128)(2,1)S(1)} %get-tuple-element.56) | copy-start | bytes 3145732
  130.1 4.5 %copy-start.25 = (bf16[256,2048]{1,0:T(8,128)(2,1)}, bf16[256,2048]{1,0:T(8,128)(2,1)S(1)}, u32[]{:S(2)}) copy-start(bf16[256,2048]{1,0:T(8,128)(2,1)S(1)} %get-tuple-element.57) | copy-start | bytes 3145732
  135.1 0.8 copy-start.6
  135.9 0.7 copy-start.15
  140.1 2.7 %copy-start.10 = (bf16[256,1024]{0,1:T(8,128)(2,1)S(1)}, bf16[256,1024]{0,1:T(8,128)(2,1)}, u32[]{:S(2)}) copy-start(bf16[256,1024]{0,1:T(8,128)(2,1)} %copy.139) | copy-start | bytes 1572868
  140.1 2.7 %copy-start.12 = (bf16[768,512]{1,0:T(8,128)(2,1)S(1)}, bf16[768,512]{1,0:T(8,128)(2,1)}, u32[]{:S(2)}) copy-start(bf16[768,512]{1,0:T(8,128)(2,1)} %copy-done.11) | copy-start | bytes 2359300
  143.4 1.0 copy-start.34
  143.4 1.0 copy-start.36
  145.9 1.0 copy-start.20
  145.9 1.0 copy-start.22
  145.9 1.4 copy-start.1
  147.7 1.5 copy-start.5
  147.7 1.5 copy-start.13
  148.1 4.2 %copy-start.16 = (bf16[256,640]{1,0:T(8,128)(2,1)S(1)}, bf16[256,640]{1,0:T(8,128)(2,1)}, u32[]{:S(2)}) copy-start(bf16[256,640]{1,0:T(8,128)(2,1)} %copy-done.15) | copy-start | bytes 983044
  148.1 4.2 %copy-start.18 = (bf16[256,4,256]{2,0,1:T(8,128)(2,1)S(1)}, bf16[256,4,256]{2,0,1:T(8,128)(2,1)}, u32[]{:S(2)}) copy-start(bf16[256,4,256]{2,0,1:T(8,128)(2,1)} %copy-done.17) | copy-start | bytes 1572868
  149.2 4.7 %copy-start.3 = (f32[256,640]{1,0:T(8,128)S(1)}, f32[256,640]{1,0:T(8,128)}, u32[]{:S(2)}) copy-start(f32[256,640]{1,0:T(8,128)} %copy-done.2) | copy-start | bytes 1966084
  149.2 4.7 %copy-start.24 = (bf16[256,2048]{1,0:T(8,128)(2,1)S(1)}, bf16[256,2048]{1,0:T(8,128)(2,1)}, u32[]{:S(2)}) copy-start(bf16[256,2048]{1,0:T(8,128)(2,1)} %copy-done.23) | copy-start | bytes 3145732
  149.2 4.7 %copy-start.26 = (bf16[256,2048]{1,0:T(8,128)(2,1)S(1)}, bf16[256,2048]{1,0:T(8,128)(2,1)}, u32[]{:S(2)}) copy-start(bf16[256,2048]{1,0:T(8,128)(2,1)} %copy-done.25) | copy-start | bytes 3145732
  149.3 8.6 %collective-permute-start.2 = (f32[256,512]{1,0:T(8,128)S(1)}, f32[256,512]{1,0:T(8,128)S(1)}, u32[]{:S(2)}, u32[]{:S(2)}) collective-permute-start(f32[256,512]{1,0:T(8,128)S(1)} %get-tuple-element.58), channel_id=1, source_target_pairs={{8,0},{16,8},{24,16},{9,1},{17,9},{25,17},{10,2},{18,10},{26,18},{... | collective-permute-start | bytes 1572872 | tf_op jit(solution)/shard_map/ppermute | solution.py:20
  150.8 21.6 %collective-permute-start.3 = (f32[256,512]{1,0:T(8,128)S(1)}, f32[256,512]{1,0:T(8,128)S(1)}, u32[]{:S(2)}, u32[]{:S(2)}) collective-permute-start(f32[256,512]{1,0:T(8,128)S(1)} %get-tuple-element.59), channel_id=1, source_target_pairs={{16,0},{24,8},{17,1},{25,9},{18,2},{26,10},{19,3},{27,11},{20,4},{... | collective-permute-start | bytes 1572872 | tf_op jit(solution)/shard_map/ppermute | solution.py:20
  157.9 17.6 %copy-start.30 = (bf16[256,4,256]{0,2,1:T(8,128)(2,1)S(1)}, bf16[256,4,256]{0,2,1:T(8,128)(2,1)}, u32[]{:S(2)}) copy-start(bf16[256,4,256]{0,2,1:T(8,128)(2,1)} %copy.115) | copy-start | bytes 1572868
  181.1 70.1 %copy-start.7 = (f32[256,640]{1,0:T(8,128)S(1)}, f32[256,640]{1,0:T(8,128)}, u32[]{:S(2)}) copy-start(f32[256,640]{1,0:T(8,128)} %copy-done.6) | copy-start | bytes 1966084
  248.4 3.8 %copy-start.32 = (f32[80,1024]{1,0:T(8,128)S(1)}, f32[80,1024]{1,0:T(8,128)}, u32[]{:S(2)}) copy-start(f32[80,1024]{1,0:T(8,128)} %get-tuple-element.111) | copy-start | bytes 983044
  248.4 4.5 %copy-start.39 = (f32[80,256]{1,0:T(8,128)S(1)}, f32[80,256]{1,0:T(8,128)}, u32[]{:S(2)}) copy-start(f32[80,256]{1,0:T(8,128)} %get-tuple-element.112) | copy-start | bytes 245764
  248.4 5.2 %copy-start.38 = (f32[80,256]{1,0:T(8,128)S(1)}, f32[80,256]{1,0:T(8,128)}, u32[]{:S(2)}) copy-start(f32[80,256]{1,0:T(8,128)} %get-tuple-element.113) | copy-start | bytes 245764
  248.4 5.8 %copy-start.31 = (f32[128,640]{1,0:T(8,128)S(1)}, f32[128,640]{1,0:T(8,128)}, u32[]{:S(2)}) copy-start(f32[128,640]{1,0:T(8,128)} %get-tuple-element.114) | copy-start | bytes 983044
  248.5 6.5 %copy-start.29 = (f32[80,2048]{1,0:T(8,128)S(1)}, f32[80,2048]{1,0:T(8,128)}, u32[]{:S(2)}) copy-start(f32[80,2048]{1,0:T(8,128)} %get-tuple-element.115) | copy-start | bytes 1966084
  251.3 4.5 %copy-start.28 = (f32[80,2048]{1,0:T(8,128)S(1)}, f32[80,2048]{1,0:T(8,128)}, u32[]{:S(2)}) copy-start(f32[80,2048]{1,0:T(8,128)} %get-tuple-element.116) | copy-start | bytes 1966084
  252.2 4.4 %copy-start.27 = (f32[256,640]{1,0:T(8,128)S(1)}, f32[256,640]{1,0:T(8,128)}, u32[]{:S(2)}) copy-start(f32[256,640]{1,0:T(8,128)} %get-tuple-element.117) | copy-start | bytes 1966084

commit v3 on v2

--- a/solution.py
+++ b/solution.py
@@ -89,10 +89,10 @@
     pl.semaphore_wait(barrier, len(peers))
 
 
-def gather_kernel(size, shapes, by_rows, shared, places, *refs):
+def gather_kernel(size, shapes, by_rows, shared, *refs):
     count = len(shapes)
-    shards, gains = refs[: len(places)], refs[len(places)]
-    refs = refs[len(places) + 1 :]
+    shards, gains = refs[:count], refs[count]
+    refs = refs[count + 1 :]
     wholes, all_gains = refs[:count], refs[count]
     own_sem, ring_send, ring_recv, pair_send, pair_recv = refs[count + 1 : count + 6]
     cross_send, cross_recv, relay_send, relay_recv = refs[count + 6 :]
@@ -105,23 +105,18 @@
     pair = (seq + way, me)
     across = (seq + 2 * (1 - 2 * plane), me)
 
-    own = []
-    for shard, (member, column) in zip(shards, places):
-        target = wholes[member].at[me, :, pl.ds(column, shard.shape[1])]
-        own.append(pltpu.make_async_copy(shard, target, own_sem.at[len(own)]))
-    own.append(pltpu.make_async_copy(gains, all_gains.at[me], own_sem.at[len(own)]))
-    for copy in own:
-        copy.start()
     greet([after, before, pair, across])
 
-    def copy_of(member, block, core, plane, sems, step, device):
+    def copy_of(member, block, core, plane, sems, step, device, first=False):
         if member == count:
             target = all_gains.at[block]
+            source = gains if first else target
         else:
             part = region(shapes[member], by_rows[member], core, plane)
             target = wholes[member].at[(block, *part)]
+            source = shards[member].at[part] if first else target
         return pltpu.make_async_remote_copy(
-            src_ref=target,
+            src_ref=source,
             dst_ref=target,
             send_sem=sems[0].at[step, member],
             recv_sem=sems[1].at[step, member],
@@ -132,8 +127,9 @@
     def plane_of(member):
         return plane if member < count and shared[member] else None
 
-    def ring_copy(member, block, step):
-        return copy_of(member, block, core, plane_of(member), (ring_send, ring_recv), step, after)
+    def ring_copy(member, block, step, first=False):
+        sems = (ring_send, ring_recv)
+        return copy_of(member, block, core, plane_of(member), sems, step, after, first)
 
     def pair_copy(member, block, step, core):
         return copy_of(member, block, core, plane_of(member), (pair_send, pair_recv), step, pair)
@@ -144,10 +140,14 @@
     def relay_copy(member, block, step, core):
         return copy_of(member, block, core, 1 - plane, (relay_send, relay_recv), step, pair)
 
+    for member in range(count + 1):
+        ring_copy(member, me, 0, first=True).start()
+    own = [
+        pltpu.make_async_copy(source, target.at[me], own_sem.at[number])
+        for number, (source, target) in enumerate(zip((*shards, gains), (*wholes, all_gains)))
+    ]
     for copy in own:
-        copy.wait()
-    for member in range(count + 1):
-        ring_copy(member, me, 0).start()
+        copy.start()
 
     def arrive(step, forward):
         block = ring_owner(place - way * step, size)
@@ -193,28 +193,24 @@
         return 0
 
     lax.fori_loop(0, size - 1, finish, 0)
-
-
-def gather_weights(shards, groups, by_rows, shared, gains):
+    for copy in own:
+        copy.wait()
+
+
+def gather_weights(shards, by_rows, shared, gains):
     size = lax.axis_size("fsdp")
-    shapes, places = [], []
-    for number, group in enumerate(groups):
-        column = 0
-        for member in group:
-            places.append((number, column))
-            column += shards[member].shape[1]
-        shapes.append((shards[group[0]].shape[0], column))
-    count = len(groups)
+    shapes = [shard.shape for shard in shards]
+    count = len(shards)
     any_space = pl.BlockSpec(memory_space=pl.ANY)
     copies = pltpu.SemaphoreType.DMA((size - 1, count + 1))
     return pl.pallas_call(
-        functools.partial(gather_kernel, size, shapes, by_rows, shared, places),
+        functools.partial(gather_kernel, size, shapes, by_rows, shared),
         out_shape=[
             jax.ShapeDtypeStruct((size, *shape), gains.dtype) for shape in (*shapes, gains.shape)
         ],
         in_specs=[any_space] * (len(shards) + 1),
         out_specs=[any_space] * (count + 1),
-        scratch_shapes=[pltpu.SemaphoreType.DMA((len(shards) + 1,)), *[copies] * 8],
+        scratch_shapes=[pltpu.SemaphoreType.DMA((count + 1,)), *[copies] * 8],
         compiler_params=pltpu.CompilerParams(collective_id=0, has_side_effects=True),
         name="gather_weights",
     )(*shards, gains)
@@ -500,19 +496,18 @@
     )(*grads, gain_grads)
 
 
-def pack_gains(members, rows, split):
-    row = jnp.concatenate([member.reshape(*split, -1) for member in members], axis=-1)
-    padding = -row.shape[-1] % 128
-    row = jnp.pad(row, [(0, 0)] * len(split) + [(0, padding)])
-    return jnp.broadcast_to(row[..., None, :], (*split, rows, row.shape[-1]))
+def pack_gains(members, rows):
+    columns = -(-max(member.shape[-1] for member in members) // 128) * 128
+    padded = [
+        jnp.pad(member, [(0, 0)] * (member.ndim - 1) + [(0, columns - member.shape[-1])])
+        for member in members
+    ]
+    padded += [jnp.zeros_like(padded[0])] * (rows - len(members))
+    return jnp.stack(padded, axis=-2)
 
 
 def unpack_gains(rows, widths):
-    pieces, start = [], 0
-    for width in widths:
-        pieces.append(rows[..., start : start + width])
-        start += width
-    return pieces
+    return [rows[..., place, :width] for place, width in enumerate(widths)]
 
 
 def on_device(
@@ -540,13 +535,16 @@
     gain_shards = (attn_norm, attn_post_norm, ffn_norm, ffn_post_norm, query_norm, key_norm)
     widths = [member.shape[0] for member in gain_shards]
     *wholes, all_gains = gather_weights(
-        shards, groups, by_rows, shared, pack_gains(gain_shards, 16, ())
+        [jnp.concatenate([shards[member] for member in group], axis=1) for group in groups],
+        by_rows,
+        shared,
+        pack_gains(gain_shards, 16),
     )
     into_w, output_w, ffn_w, down_w = (whole.reshape(-1, whole.shape[-1]) for whole in wholes)
     query_width, head_width = query_proj.shape[1], key_proj.shape[1]
     ffn_width = gate_proj.shape[1]
     attn_gain, attn_post_gain, ffn_gain, ffn_post_gain, query_gain, key_gain = (
-        piece.reshape(-1).astype(jnp.float32) for piece in unpack_gains(all_gains[:, 0], widths)
+        piece.reshape(-1).astype(jnp.float32) for piece in unpack_gains(all_gains, widths)
     )
     source = inputs[0].astype(jnp.float32)
     tokens = source.shape[0]
@@ -683,16 +681,15 @@
         grad.astype(jnp.bfloat16).reshape(size, -1, grad.shape[-1])
         for grad in (into_grad, output_grad, ffn_grad, down_grad)
     ]
-    gain_grads = pack_gains(
-        (grad_pre1, grad_post1, grad_pre2, grad_post2, grad_qgain, grad_kgain), 8, (size,)
-    )
+    local = (grad_pre1, grad_post1, grad_pre2, grad_post2, grad_qgain, grad_kgain)
+    gain_grads = pack_gains([member.reshape(size, -1) for member in local], 8)
     piece_widths = [[shards[member].shape[1] for member in group] for group in groups]
     *results, gain_total = reduce_grads(grads, piece_widths, by_rows, shared, gain_grads)
     return (
         result.astype(jnp.bfloat16)[None],
         grad_input.astype(jnp.bfloat16)[None],
         *results,
-        *unpack_gains(gain_total[0], widths),
+        *unpack_gains(gain_total, widths),
     )
 
 

time: 258 us -> 214 us (0.83)
  Pallas kernels: 161 us -> 122 us
  waiting for transfers between devices: 17.6 us -> 8.88 us
  other arithmetic: 13.8 us -> 21.1 us
    pallas_call x1, Pallas kernels: 93.9 us -> 51.2 us  [gather_weights(): pl.pallas_call(functools.partial(gather_kernel, size, shapes, by_rows, sh...]
    ppermute x4, waiting for transfers between devices: 17.6 us -> 8.88 us  [shifted(): return lax.ppermute(array, axis, pairs)]
    concatenate x2 -> x0, local copies, waits for them, and re-layouts: 4.18 us -> none  [pack_gains(): jnp.concatenate([member.reshape(*split, -1) for member in members], axis=-1)]
    another operation x0 -> x8, local copies, waits for them, and re-layouts: none -> 3.89 us  [pack_gains(): return jnp.stack(padded, axis=-2)]
    concatenate x0 -> x2, other arithmetic: none -> 3.67 us  [on_device(): jnp.concatenate([shards[member] for member in group], axis=1)]
    slice x3 -> x0, local copies, waits for them, and re-layouts: 3.58 us -> none  [the longest x2 2.77 us: unpack_gains(): pieces.append(rows[..., start:start + width])]
    pallas_call x1, Pallas kernels: 67.3 us -> 70.5 us  [reduce_grads(): pl.pallas_call(functools.partial(reduce_kernel, size, blocks, shapes, by_...]
    squeeze x0 -> x2, local copies, waits for them, and re-layouts: none -> 2.63 us  [unpack_gains(): return [rows[..., place, :width] for place, width in enumerate(widths)]]
  transfers between devices with their start and end apart: 4 -> 4, of which waited for: 2 -> 2; matrix products, arithmetic and copies ran while one was open for 3% -> 5% of each run, Pallas kernels for 0% -> 0%
where the time goes in v3:
time: 214 us; the launch traced here: 213 us
  Pallas kernels  122 us (57%)
  matrix products  29.6 us (14%)
  local copies, waits for them, and re-layouts  21.8 us (10%)
  other arithmetic  21.1 us (10%)
  waiting for transfers between devices  8.88 us (4%)
  starting transfers between devices  8.17 us (4%)
    pallas_call x1, Pallas kernels, reduce_grads(): pl.pallas_call(functools.partial(reduce_kernel, size, blocks, shapes, by_...  70.5 us
    pallas_call x1, Pallas kernels, gather_weights(): pl.pallas_call(functools.partial(gather_kernel, size, shapes, by_rows, sh...  51.2 us
    unnamed x101, local copies, waits for them, and re-layouts  10.4 us
    dot_general x4, matrix products, row_outer(): lax.dot_general(left, right, (((0,), (0,)), ((), ())), preferred_element_...  10.2 us
    ppermute x4, waiting for transfers between devices, shifted(): return lax.ppermute(array, axis, pairs)  8.88 us
    ppermute x4, starting transfers between devices, shifted(): return lax.ppermute(array, axis, pairs)  8.17 us
    dot_general x4, matrix products, back_product(): lax.dot_general(grad_rows, weight, (((1,), (1,)), ((), ())), preferred_el...  8.17 us
  transfers between devices with their start and end apart: 4, of which 2 were waited for; matrix products, arithmetic and copies ran while one was open for 5% of the time, Pallas kernels for 0%

profile of v3, /device:TPU:0, one launch (start us, length us, event | category | flops | bytes accessed | tf_op | source)
XLA Modules:
  0.0 212.8 jit_solution(839160875357266457)
XLA Ops:
  0.7 2.0 pad_maximum_fusion.4.refs_2_
  4.7 1.7 pad_maximum_fusion.12.refs_0_
  6.4 1.2 stack.59.refs_4_
  7.5 51.2 %gather_weights.1 = (bf16[8,80,1536]{2,1,0:T(8,128)(2,1)}, bf16[8,128,640]{2,1,0:T(8,128)(2,1)}, bf16[8,80,4096]{2,1,0:T(8,128)(2,1)}, bf16[8,256,640]{2,1,0:T(8,128)(2,1)}, bf16[8,16,128]{2,1,0:T(8,128)(2,1)}) custom-call(bf16[80,1536]{1,0:T(8,128)(2,1)} %pad_maximum_fusion.12.refs_0_, bf16[128,640]{1,0:T(8,128)(2,1)} %refs_1_.1, ...), custom_call_target="tpu_custom_call" | custom-call | tf_op jit(solution)/shard_map/gather_weights/pallas_call | solution.py:206
  58.8 0.9 convert_reduce_fusion
  59.7 0.8 convert_reduce_fusion.4
  60.8 2.4 %fusion.56 = f32[256,1536]{1,0:T(8,128)S(1)} fusion(bf16[640,1536]{1,0:T(8,128)(2,1)} %bitcast.173, bf16[1,256,640]{2,1,0:T(8,128)(2,1)S(1)} %copy-done.9, f32[640]{0:T(1024)S(1)} %reshape.405, f32[256]{0:T(256)S(1)} %fusion.81), kind=kOutput, calls=%fused_computation.115 | convolution fusion | flops 503971840 | bytes 3870208 | tf_op jit(solution)/shard_map/dot_general | solution.py:558
  64.1 0.8 pad_maximum_fusion.11
  64.9 3.0 %collective-permute-start.1 = (bf16[256,512]{1,0:T(8,128)(2,1)}, bf16[256,512]{1,0:T(8,128)(2,1)}, u32[]{:S(2)}, u32[]{:S(2)}) collective-permute-start(bf16[256,512]{1,0:T(8,128)(2,1)} %pad_maximum_fusion.11), channel_id=1, source_target_pairs={{0,8},{8,16},{16,24},{1,9},{9,17},{17,25},{2,10},{10,18},{18,26},{... | collective-permute-start | bytes 786440 | tf_op jit(solution)/shard_map/ppermute | solution.py:20
  67.9 2.4 %collective-permute-start = (bf16[256,512]{1,0:T(8,128)(2,1)}, bf16[256,512]{1,0:T(8,128)(2,1)}, u32[]{:S(2)}, u32[]{:S(2)}) collective-permute-start(bf16[256,512]{1,0:T(8,128)(2,1)} %pad_maximum_fusion.11), channel_id=1, source_target_pairs={{0,16},{8,24},{1,17},{9,25},{2,18},{10,26},{3,19},{11,27},{4,20},{... | collective-permute-start | bytes 786440 | tf_op jit(solution)/shard_map/ppermute | solution.py:20
  71.7 1.0 fusion.32
  73.1 3.5 %collective-permute-done = bf16[256,512]{1,0:T(8,128)(2,1)} collective-permute-done((bf16[256,512]{1,0:T(8,128)(2,1)}, bf16[256,512]{1,0:T(8,128)(2,1)}, u32[]{:S(2)}, u32[]{:S(2)}) %collective-permute-start) | collective-permute-done | bytes 262176 | tf_op jit(solution)/shard_map/ppermute | solution.py:20
  76.6 1.1 maximum_maximum_fusion
  79.6 0.8 copy-done.10
  81.4 1.9 fusion.93
  83.3 0.7 multiply_convert_fusion.1
  84.1 1.1 copy-done.44
  85.2 1.1 multiply_reduce_fusion.6
  86.6 1.0 fusion.44
  87.6 2.3 %fusion.11 = (bf16[256,2048]{1,0:T(8,128)(2,1)S(1)}, bf16[256,2048]{1,0:T(8,128)(2,1)S(1)}) fusion(f32[256,4096]{1,0:T(8,128)S(1)} %fusion.93, bf16[256,640]{1,0:T(8,128)(2,1)S(1)} %get-tuple-element.70, bf16[2048,640]{1,0:T(8,128)(2,1)S(1)} %bitcast.185), kind=kOutput, calls=%fused_computation.22 | convolution fusion | flops 683671552 | bytes 9240576 | tf_op jit(solution)/shard_map/dot_general | solution.py:51
  90.0 1.9 multiply_reduce_fusion.2
  93.3 0.7 copy-done.17
  94.0 1.4 convolution_convert_fusion.4
  95.4 2.0 copy.138
  97.4 1.9 fusion
  102.4 0.7 fusion.16
  103.7 2.5 %convolution_convert_fusion.1 = bf16[2048,640]{1,0:T(8,128)(2,1)} fusion(bf16[256,2048]{1,0:T(8,128)(2,1)S(1)} %copy-done.13, bf16[256,640]{1,0:T(8,128)(2,1)S(1)} %copy-done.22), kind=kOutput, calls=%fused_computation.1 | convolution fusion | flops 672399360 | bytes 3997696 | tf_op jit(solution)/shard_map/dot_general | solution.py:45
  106.2 1.1 fusion.49
  107.4 1.3 collective-permute-start.3
  108.7 1.5 collective-permute-start.2
  111.2 1.0 copy.115
  112.5 1.7 convolution_convert_fusion.3
  114.2 3.9 %convolution_convert_fusion = bf16[640,4096]{1,0:T(8,128)(2,1)} fusion(bf16[256,2048]{1,0:T(8,128)(2,1)S(1)} %copy-done.30, bf16[256,2048]{1,0:T(8,128)(2,1)S(1)} %copy-done.28, f32[256,640]{1,0:T(8,128)S(1)} %copy-done.3, f32[640]{0:T(1024)S(1)} %reshape.409, f32[256]{0:T(256)S(1)} %fusion.84), kind=kOutput, calls=%fused_computation | convolution fusion | flops 1349484544 | bytes 7998976 | tf_op jit(solution)/shard_map/dot_general | solution.py:45
  118.1 5.4 %collective-permute-done.3 = f32[256,512]{1,0:T(8,128)} collective-permute-done((f32[256,512]{1,0:T(8,128)}, f32[256,512]{1,0:T(8,128)}, u32[]{:S(2)}, u32[]{:S(2)}) %collective-permute-start.3) | collective-permute-done | bytes 524320 | tf_op jit(solution)/shard_map/ppermute | solution.py:20
  123.5 1.3 fusion.52
  125.6 1.1 multiply_reduce_fusion.9
  126.7 1.1 fusion.65
  127.9 2.5 %fusion.39 = (f32[640]{0:T(1024)S(1)}, f32[256]{0:T(256)S(1)}, f32[256,640]{1,0:T(8,128)S(1)}) fusion(bf16[1,256,640]{2,1,0:T(8,128)(2,1)S(1)} %copy-done.9, f32[256]{0:T(256)S(1)} %fusion.81, f32[640]{0:T(1024)S(1)} %reshape.405, bf16[640,1536]{1,0:T(8,128)(2,1)} %bitcast.174, bf16[256,256]{0,1:T(8,128)(2,1)S(1)} %copy.123, ...), kind=kOutput, calls=%fused_computation.79 | convolution fusion | flops 506821760 | bytes 3742720 | tf_op jit(solution)/shard_map/dot_general | solution.py:51
  130.4 2.1 %convolution_convert_fusion.2 = bf16[640,1536]{1,0:T(8,128)(2,1)} fusion(bf16[1,256,640]{2,1,0:T(8,128)(2,1)S(1)} %copy-done.9, f32[256]{0:T(256)S(1)} %fusion.81, f32[640]{0:T(1024)S(1)} %reshape.405, bf16[256,256]{0,1:T(8,128)(2,1)S(1)} %copy.123, bf16[256,256]{0,1:T(8,128)(2,1)S(1)} %copy.122, bf16[256,1024]{0,1:T(8,128)(2,1)S(1)} %bitcast.177), kind=kOutput, calls=%fused_computation.2 | convolution fusion | flops 507314176 | bytes 3083776 | tf_op jit(solution)/shard_map/dot_general | solution.py:45
  133.4 70.5 %reduce_grads.1 = (f32[80,1024]{1,0:T(8,128)}, f32[80,256]{1,0:T(8,128)}, f32[80,256]{1,0:T(8,128)}, f32[128,640]{1,0:T(8,128)}, f32[80,2048]{1,0:T(8,128)}, /*i...) custom-call(bf16[8,80,1536]{2,1,0:T(8,128)(2,1)} %bitcast.175, bf16[8,128,640]{2,1,0:T(8,128)(2,1)} %bitcast.168, ...), custom_call_target="tpu_custom_call" | custom-call | tf_op jit(solution)/shard_map/reduce_grads/pallas_call | solution.py:459
  203.9 1.4 slice_bitcast_fusion.8
  205.3 1.3 slice_bitcast_fusion.6
  206.6 0.9 fusion.54
  207.5 0.7 copy.151
  209.5 0.7 copy.154
  210.3 0.8 copy.155
  211.1 0.8 copy.156
  212.0 0.8 copy.157
  (168 shorter events, 17.2 us)
Async XLA Ops:
  0.6 60.0 %copy-start.9 = (bf16[1,256,640]{2,1,0:T(8,128)(2,1)S(1)}, bf16[1,256,640]{2,1,0:T(8,128)(2,1)}, u32[]{:S(2)}) copy-start(bf16[1,256,640]{2,1,0:T(8,128)(2,1)} %param.15) | copy-start | bytes 983044
  63.2 7.2 %copy-start.4 = (f32[256,1536]{1,0:T(8,128)}, f32[256,1536]{1,0:T(8,128)S(1)}, u32[]{:S(2)}) copy-start(f32[256,1536]{1,0:T(8,128)S(1)} %fusion.56) | copy-start | bytes 4718596
  64.1 8.8 %copy-start.23 = (f32[256,128]{1,0:T(8,128)}, f32[256,128]{1,0:T(8,128)S(1)}, u32[]{:S(2)}) copy-start(f32[256,128]{1,0:T(8,128)S(1)} %get-tuple-element.82) | copy-start | bytes 393220
  64.1 8.8 %copy-start.25 = (f32[256,128]{1,0:T(8,128)}, f32[256,128]{1,0:T(8,128)S(1)}, u32[]{:S(2)}) copy-start(f32[256,128]{1,0:T(8,128)S(1)} %get-tuple-element.83) | copy-start | bytes 393220
  64.9 8.2 %collective-permute-start.1 = (bf16[256,512]{1,0:T(8,128)(2,1)}, bf16[256,512]{1,0:T(8,128)(2,1)}, u32[]{:S(2)}, u32[]{:S(2)}) collective-permute-start(bf16[256,512]{1,0:T(8,128)(2,1)} %pad_maximum_fusion.11), channel_id=1, source_target_pairs={{0,8},{8,16},{16,24},{1,9},{9,17},{17,25},{2,10},{10,18},{18,26},{... | collective-permute-start | bytes 786440 | tf_op jit(solution)/shard_map/ppermute | solution.py:20
  67.9 8.7 %collective-permute-start = (bf16[256,512]{1,0:T(8,128)(2,1)}, bf16[256,512]{1,0:T(8,128)(2,1)}, u32[]{:S(2)}, u32[]{:S(2)}) collective-permute-start(bf16[256,512]{1,0:T(8,128)(2,1)} %pad_maximum_fusion.11), channel_id=1, source_target_pairs={{0,16},{8,24},{1,17},{9,25},{2,18},{10,26},{3,19},{11,27},{4,20},{... | collective-permute-start | bytes 786440 | tf_op jit(solution)/shard_map/ppermute | solution.py:20
  70.4 1.3 copy-start
  72.9 4.8 %copy-start.41 = (pred[256,768]{0,1:T(8,128)(4,1)S(1)}, pred[256,768]{0,1:T(8,128)(4,1)}, u32[]{:S(2)}) copy-start(pred[256,768]{0,1:T(8,128)(4,1)} %fusion.32) | copy-start | bytes 589828
  73.1 5.3 %copy-start.37 = (bf16[256,4,128]{2,0,1:T(8,128)(2,1)}, bf16[256,4,128]{2,0,1:T(8,128)(2,1)S(1)}, u32[]{:S(2)}) copy-start(bf16[256,4,128]{2,0,1:T(8,128)(2,1)S(1)} %get-tuple-element.68) | copy-start | bytes 786436
  73.1 5.3 %copy-start.39 = (bf16[256,4,128]{2,0,1:T(8,128)(2,1)}, bf16[256,4,128]{2,0,1:T(8,128)(2,1)S(1)}, u32[]{:S(2)}) copy-start(bf16[256,4,128]{2,0,1:T(8,128)(2,1)S(1)} %get-tuple-element.69) | copy-start | bytes 786436
  77.7 1.2 copy-start.14
  78.4 3.0 %slice-start = ((s8[5242880]{0:T(1024)(128)(4,1)}), s8[4194304]{0:T(1024)(128)(4,1)S(1)}, s32[]{:S(2)}) async-start(s8[5242880]{0:T(1024)(128)(4,1)} %bitcast.162), calls=%async_computation | async-start | bytes 8388608
  78.8 1.5 copy-start.10
  78.8 2.6 %slice-start.1 = ((s8[5242880]{0:T(1024)(128)(4,1)}), s8[1048576]{0:T(1024)(128)(4,1)S(1)}, s32[]{:S(2)}) async-start(s8[5242880]{0:T(1024)(128)(4,1)} %bitcast.162), calls=%async_computation.1 | async-start | bytes 2097152
  79.5 1.8 copy-start.19
  81.4 10.6 %copy-start.2 = (f32[256,640]{1,0:T(8,128)}, f32[256,640]{1,0:T(8,128)S(1)}, u32[]{:S(2)}) copy-start(f32[256,640]{1,0:T(8,128)S(1)} %get-tuple-element.61) | copy-start | bytes 1966084
  83.3 1.8 copy-start.44
  84.1 2.2 %copy-start.12 = (bf16[256,2048]{1,0:T(8,128)(2,1)}, bf16[256,2048]{1,0:T(8,128)(2,1)S(1)}, u32[]{:S(2)}) copy-start(bf16[256,2048]{1,0:T(8,128)(2,1)S(1)} %multiply_convert_fusion.1) | copy-start | bytes 3145732
  87.6 2.3 %copy-start.21 = (bf16[256,640]{1,0:T(8,128)(2,1)}, bf16[256,640]{1,0:T(8,128)(2,1)S(1)}, u32[]{:S(2)}) copy-start(bf16[256,640]{1,0:T(8,128)(2,1)S(1)} %get-tuple-element.70) | copy-start | bytes 983044
  89.9 2.0 copy-start.27
  89.9 2.0 copy-start.29
  97.4 1.9 copy-start.11
  99.9 6.3 %copy-start.5 = (f32[768,256]{1,0:T(8,128)}, f32[768,256]{1,0:T(8,128)S(1)}, u32[]{:S(2)}) copy-start(f32[768,256]{1,0:T(8,128)S(1)} %fusion.19) | copy-start | bytes 2359300
  100.0 1.1 copy-start.38
  100.0 1.3 copy-start.40
  101.3 1.1 copy-start.15
  102.4 1.2 copy-start.13
  102.4 1.3 copy-start.22
  106.2 4.0 %copy-start.24 = (f32[256,128]{1,0:T(8,128)S(1)}, f32[256,128]{1,0:T(8,128)}, u32[]{:S(2)}) copy-start(f32[256,128]{1,0:T(8,128)} %copy-done.23) | copy-start | bytes 393220
  106.2 4.0 %copy-start.26 = (f32[256,128]{1,0:T(8,128)S(1)}, f32[256,128]{1,0:T(8,128)}, u32[]{:S(2)}) copy-start(f32[256,128]{1,0:T(8,128)} %copy-done.25) | copy-start | bytes 393220
  106.2 4.1 %copy-start.1 = (f32[256,1024]{1,0:T(8,128)S(1)}, f32[256,1024]{1,0:T(8,128)}, u32[]{:S(2)}) copy-start(f32[256,1024]{1,0:T(8,128)} %copy-done) | copy-start | bytes 3145732
  107.4 16.2 %collective-permute-start.3 = (f32[256,512]{1,0:T(8,128)}, f32[256,512]{1,0:T(8,128)}, u32[]{:S(2)}, u32[]{:S(2)}) collective-permute-start(f32[256,512]{1,0:T(8,128)} %get-tuple-element.65), channel_id=1, source_target_pairs={{16,0},{24,8},{17,1},{25,9},{18,2},{26,10},{19,3},{27,11},{20,4},{... | collective-permute-start | bytes 1572872 | tf_op jit(solution)/shard_map/ppermute | solution.py:20
  108.7 14.9 %collective-permute-start.2 = (f32[256,512]{1,0:T(8,128)}, f32[256,512]{1,0:T(8,128)}, u32[]{:S(2)}, u32[]{:S(2)}) collective-permute-start(f32[256,512]{1,0:T(8,128)} %get-tuple-element.64), channel_id=1, source_target_pairs={{8,0},{16,8},{24,16},{9,1},{17,9},{25,17},{10,2},{18,10},{26,18},{... | collective-permute-start | bytes 1572872 | tf_op jit(solution)/shard_map/ppermute | solution.py:20
  110.8 1.8 copy-start.18
  110.8 1.8 copy-start.20
  111.2 3.0 %copy-start.3 = (f32[256,640]{1,0:T(8,128)S(1)}, f32[256,640]{1,0:T(8,128)}, u32[]{:S(2)}) copy-start(f32[256,640]{1,0:T(8,128)} %copy-done.2) | copy-start | bytes 1966084
  112.5 1.7 copy-start.28
  112.5 1.7 copy-start.30
  114.2 9.3 %copy-start.6 = (f32[768,256]{1,0:T(8,128)S(1)}, f32[768,256]{1,0:T(8,128)}, u32[]{:S(2)}) copy-start(f32[768,256]{1,0:T(8,128)} %copy-done.5) | copy-start | bytes 2359300
  118.1 9.8 %copy-start.34 = (bf16[256,4,256]{0,2,1:T(8,128)(2,1)S(1)}, bf16[256,4,256]{0,2,1:T(8,128)(2,1)}, u32[]{:S(2)}) copy-start(bf16[256,4,256]{0,2,1:T(8,128)(2,1)} %copy.115) | copy-start | bytes 1572868
  133.4 73.2 %copy-start.8 = (f32[256,640]{1,0:T(8,128)S(1)}, f32[256,640]{1,0:T(8,128)}, u32[]{:S(2)}) copy-start(f32[256,640]{1,0:T(8,128)} %copy-done.7) | copy-start | bytes 1966084
  203.9 3.7 %copy-start.36 = (f32[80,1024]{1,0:T(8,128)S(1)}, f32[80,1024]{1,0:T(8,128)}, u32[]{:S(2)}) copy-start(f32[80,1024]{1,0:T(8,128)} %get-tuple-element.117) | copy-start | bytes 983044
  203.9 4.4 %copy-start.43 = (f32[80,256]{1,0:T(8,128)S(1)}, f32[80,256]{1,0:T(8,128)}, u32[]{:S(2)}) copy-start(f32[80,256]{1,0:T(8,128)} %get-tuple-element.118) | copy-start | bytes 245764
  203.9 5.0 %copy-start.42 = (f32[80,256]{1,0:T(8,128)S(1)}, f32[80,256]{1,0:T(8,128)}, u32[]{:S(2)}) copy-start(f32[80,256]{1,0:T(8,128)} %get-tuple-element.119) | copy-start | bytes 245764
  203.9 5.6 %copy-start.35 = (f32[128,640]{1,0:T(8,128)S(1)}, f32[128,640]{1,0:T(8,128)}, u32[]{:S(2)}) copy-start(f32[128,640]{1,0:T(8,128)} %get-tuple-element.120) | copy-start | bytes 983044
  203.9 6.4 %copy-start.33 = (f32[80,2048]{1,0:T(8,128)S(1)}, f32[80,2048]{1,0:T(8,128)}, u32[]{:S(2)}) copy-start(f32[80,2048]{1,0:T(8,128)} %get-tuple-element.121) | copy-start | bytes 1966084
  206.6 4.5 %copy-start.32 = (f32[80,2048]{1,0:T(8,128)S(1)}, f32[80,2048]{1,0:T(8,128)}, u32[]{:S(2)}) copy-start(f32[80,2048]{1,0:T(8,128)} %get-tuple-element.122) | copy-start | bytes 1966084
  207.5 4.4 %copy-start.31 = (f32[256,640]{1,0:T(8,128)S(1)}, f32[256,640]{1,0:T(8,128)}, u32[]{:S(2)}) copy-start(f32[256,640]{1,0:T(8,128)} %get-tuple-element.123) | copy-start | bytes 1966084
  (3 other events, 2.7 us)

commit v4 on v3

--- a/solution.py
+++ b/solution.py
@@ -225,14 +225,15 @@
         del every[:number]
         return taken
 
-    mine, (gain_mine,) = take(count), take(1)
+    grads, (gain_mine,) = take(count), take(1)
     results, (gain_total,) = take(len(places)), take(1)
-    totals, parts, landed, crossed = take(count), take(count), take(count), take(count)
+    totals, mine, parts = take(count), take(count), take(count)
+    landed, crossed = take(count), take(count)
     spread, agreed = take(count), take(count)
     gain_sent, gain_landed, gain_spread = take(3)
     pair_send, pair_recv, ring_send, ring_recv, cross_send, cross_recv = take(6)
     spread_send, spread_recv, gain_send, gain_recv = take(4)
-    agree_send, agree_recv, last_send, last_recv = take(4)
+    agree_send, agree_recv, last_send, last_recv, own_sem = take(5)
 
     seq, me = lax.axis_index("seq"), lax.axis_index("fsdp")
     core, plane = lax.rem(seq, 2), lax.rem(seq // 2, 2)
@@ -265,14 +266,18 @@
     def ring_part(member):
         return within(member, plane) if shared[member] else (slice(None), slice(None))
 
-    def own_part(member, part):
-        return region(shapes[member], by_rows[member], core, part if shared[member] else None)
+    def own_copy(member, step):
+        part = region(shapes[member], by_rows[member], core)
+        source = grads[member].at[(block_at(step), *part)]
+        return pltpu.make_async_copy(
+            source, mine[member].at[block_at(step)], own_sem.at[step, member]
+        )
 
     def pair_copy(member, step):
         block = ring_owner(place + way * (1 + step), size)
         part = region(shapes[member], by_rows[member], 1 - core)
         return remote(
-            mine[member].at[(block, *part)],
+            grads[member].at[(block, *part)],
             parts[member].at[block],
             (pair_send, pair_recv),
             (step, member),
@@ -295,6 +300,7 @@
 
     def start_pair(step, _):
         for member in range(count):
+            own_copy(member, step).start()
             pair_copy(member, step).start()
         return 0
 
@@ -303,10 +309,11 @@
     def prepare(step):
         block = block_at(step)
         for member in range(count):
+            own_copy(member, step).wait()
             pair_copy(member, step).wait_recv()
             if shared[member]:
                 spot = (block, *within(member, 1 - plane))
-                total = mine[member][(block, *own_part(member, 1 - plane))].astype(jnp.float32)
+                total = mine[member][spot].astype(jnp.float32)
                 total = total + parts[member][spot].astype(jnp.float32)
                 parts[member][spot] = total.astype(jnp.bfloat16)
                 cross_copy(member, step).start()
@@ -315,7 +322,7 @@
         block = block_at(step)
         for member in range(count):
             spot = (block, *ring_part(member))
-            total = mine[member][(block, *own_part(member, plane))].astype(jnp.float32)
+            total = mine[member][spot].astype(jnp.float32)
             total = total + parts[member][spot].astype(jnp.float32)
             if shared[member]:
                 cross_copy(member, step).wait_recv()
@@ -459,10 +466,11 @@
     return pl.pallas_call(
         functools.partial(reduce_kernel, size, blocks, shapes, by_rows, shared, places),
         out_shape=[jax.ShapeDtypeStruct(shape, jnp.float32) for shape in (*results, gain_shape)],
-        in_specs=[in_vmem] * (count + 1),
+        in_specs=[pl.BlockSpec(memory_space=pl.ANY)] * count + [in_vmem],
         out_specs=[in_vmem] * (len(results) + 1),
         scratch_shapes=[
             *[pltpu.VMEM(shape, jnp.float32) for shape in shapes],
+            *buffers([(size,)] * count, halves),
             *buffers([(size,)] * count, halves),
             *buffers([(size - 1,)] * count, pieces),
             *buffers(
@@ -488,6 +496,7 @@
             dma((count,)),
             dma((count,)),
             dma((count,)),
+            dma((size, count)),
         ],
         compiler_params=pltpu.CompilerParams(
             collective_id=1, has_side_effects=True, vmem_limit_bytes=VMEM_BYTES
@@ -531,7 +540,7 @@
     shards = (query_proj, key_proj, value_proj, output_proj, gate_proj, up_proj, down_proj)
     groups = ((0, 1, 2), (3,), (4, 5), (6,))
     by_rows = (False, True, False, True)
-    shared = (False, True, True, False)
+    shared = (True, False, True, False)
     gain_shards = (attn_norm, attn_post_norm, ffn_norm, ffn_post_norm, query_norm, key_norm)
     widths = [member.shape[0] for member in gain_shards]
     *wholes, all_gains = gather_weights(
@@ -593,7 +602,6 @@
     raised = jnp.exp(masked - row_max)
     row_sum = jnp.sum(raised, axis=-1, keepdims=True)
     attn_prob = raised / row_sum
-    log_total = row_max + jnp.log(row_sum)
     attended = jnp.einsum(
         "hqk,kd->qhd",
         attn_prob.astype(jnp.bfloat16),
@@ -638,14 +646,9 @@
         .astype(jnp.bfloat16)
         .reshape(tokens, head_count, head_width)
     )
-    scores_again = (
-        jnp.einsum("qhd,kd->hqk", query_low, keys_ext, preferred_element_type=jnp.float32)
-        * score_scale
-    )
-    prob_again = jnp.exp(jnp.where(allowed, scores_again, -1e30) - log_total)
     grad_prob = jnp.einsum("qhd,kd->hqk", grad_att, values_ext, preferred_element_type=jnp.float32)
-    inner_sum = jnp.sum(prob_again * grad_prob, axis=-1, keepdims=True)
-    grad_scores = (prob_again * (grad_prob - inner_sum)).astype(jnp.bfloat16)
+    inner_sum = jnp.sum(attn_prob * grad_prob, axis=-1, keepdims=True)
+    grad_scores = (attn_prob * (grad_prob - inner_sum)).astype(jnp.bfloat16)
     grad_query = (
         jnp.einsum("hqk,kd->qhd", grad_scores, keys_ext, preferred_element_type=jnp.float32)
         * score_scale
@@ -655,7 +658,7 @@
         * score_scale
     )
     grad_values_ext = jnp.einsum(
-        "hqk,qhd->kd", prob_again.astype(jnp.bfloat16), grad_att, preferred_element_type=jnp.float32
+        "hqk,qhd->kd", attn_prob.astype(jnp.bfloat16), grad_att, preferred_element_type=jnp.float32
     )
     grad_pairs = jnp.concatenate([grad_keys_ext, grad_values_ext], axis=1)
     own_grad = grad_pairs[hop_count * tokens :]

time: 214 us -> 216 us (level)
  waiting for transfers between devices: 8.88 us -> 1.32 us
  local copies, waits for them, and re-layouts: 21.8 us -> 28.1 us
  other arithmetic: 21.1 us -> 26.4 us
  Pallas kernels: 122 us -> 117 us
  matrix products: 29.6 us -> 32.7 us
    ppermute x4, waiting for transfers between devices: 8.88 us -> 1.32 us  [shifted(): return lax.ppermute(array, axis, pairs)]
    unnamed x101 -> x151, local copies, waits for them, and re-layouts: 10.4 us -> 14 us
    pallas_call x1, Pallas kernels: 70.5 us -> 67.3 us  [reduce_grads(): pl.pallas_call(functools.partial(reduce_kernel, size, blocks, shapes, by_...]
  transfers between devices with their start and end apart: 4 -> 4, of which waited for: 2 -> 1; matrix products, arithmetic and copies ran while one was open for 5% -> 9% of each run, Pallas kernels for 0% -> 0%
where the time goes in v4:
time: 216 us; the launch traced here: 215 us
  Pallas kernels  117 us (54%)
  matrix products  32.7 us (15%)
  local copies, waits for them, and re-layouts  28.1 us (13%)
  other arithmetic  26.4 us (12%)
  starting transfers between devices  8.42 us (4%)
    pallas_call x1, Pallas kernels, reduce_grads(): pl.pallas_call(functools.partial(reduce_kernel, size, blocks, shapes, by_...  67.3 us
    pallas_call x1, Pallas kernels, gather_weights(): pl.pallas_call(functools.partial(gather_kernel, size, shapes, by_rows, sh...  49.5 us
    unnamed x151, local copies, waits for them, and re-layouts  14 us
    dot_general x4, matrix products, row_outer(): lax.dot_general(left, right, (((0,), (0,)), ((), ())), preferred_element_...  11.6 us
    dot_general x4, matrix products, back_product(): lax.dot_general(grad_rows, weight, (((1,), (1,)), ((), ())), preferred_el...  8.99 us
    ppermute x4, starting transfers between devices, shifted(): return lax.ppermute(array, axis, pairs)  8.42 us
  transfers between devices with their start and end apart: 4, of which 1 were waited for; matrix products, arithmetic and copies ran while one was open for 9% of the time, Pallas kernels for 0%

profile of v4, /device:TPU:0, one launch (start us, length us, event | category | flops | bytes accessed | tf_op | source)
XLA Modules:
  0.0 215.3 jit_solution(2008635730996804020)
XLA Ops:
  0.7 2.0 pad_maximum_fusion.4.refs_2_
  4.7 1.7 pad_maximum_fusion.12.refs_0_
  6.4 1.2 stack.59.refs_4_
  7.6 49.5 %gather_weights.1 = (bf16[8,80,1536]{2,1,0:T(8,128)(2,1)}, bf16[8,128,640]{2,1,0:T(8,128)(2,1)}, bf16[8,80,4096]{2,1,0:T(8,128)(2,1)}, bf16[8,256,640]{2,1,0:T(8,128)(2,1)}, bf16[8,16,128]{2,1,0:T(8,128)(2,1)}) custom-call(bf16[80,1536]{1,0:T(8,128)(2,1)} %pad_maximum_fusion.12.refs_0_, bf16[128,640]{1,0:T(8,128)(2,1)} %refs_1_.1, ...), custom_call_target="tpu_custom_call" | custom-call | tf_op jit(solution)/shard_map/gather_weights/pallas_call | solution.py:206
  57.0 1.5 convert_reduce_fusion
  58.6 0.8 convert_reduce_fusion.3
  59.6 2.4 %fusion.54 = f32[256,1536]{1,0:T(8,128)S(1)} fusion(bf16[640,1536]{1,0:T(8,128)(2,1)} %bitcast.178, bf16[1,256,640]{2,1,0:T(8,128)(2,1)S(1)} %copy-done.2, f32[640]{0:T(1024)S(1)} %reshape.397, f32[256]{0:T(256)S(1)} %fusion.79), kind=kOutput, calls=%fused_computation.117 | convolution fusion | flops 503971840 | bytes 3870208 | tf_op jit(solution)/shard_map/dot_general | solution.py:567
  64.3 3.0 %collective-permute-start.1 = (bf16[256,512]{1,0:T(8,128)(2,1)}, bf16[256,512]{1,0:T(8,128)(2,1)}, u32[]{:S(2)}, u32[]{:S(2)}) collective-permute-start(bf16[256,512]{1,0:T(8,128)(2,1)} %pad_maximum_fusion.11), channel_id=1, source_target_pairs={{0,8},{8,16},{16,24},{1,9},{9,17},{17,25},{2,10},{10,18},{18,26},{... | collective-permute-start | bytes 786440 | tf_op jit(solution)/shard_map/ppermute | solution.py:20
  67.2 2.6 %collective-permute-start = (bf16[256,512]{1,0:T(8,128)(2,1)}, bf16[256,512]{1,0:T(8,128)(2,1)}, u32[]{:S(2)}, u32[]{:S(2)}) collective-permute-start(bf16[256,512]{1,0:T(8,128)(2,1)} %pad_maximum_fusion.11), channel_id=1, source_target_pairs={{0,16},{8,24},{1,17},{9,25},{2,18},{10,26},{3,19},{11,27},{4,20},{... | collective-permute-start | bytes 786440 | tf_op jit(solution)/shard_map/ppermute | solution.py:20
  70.1 1.5 reshape.381
  71.6 1.6 multiply_reduce_fusion.1
  73.3 1.2 fusion.20
  74.5 1.0 fusion.29
  76.3 1.3 subtract_convert_fusion
  77.7 1.3 maximum_maximum_fusion
  80.1 1.6 fusion.95
  82.4 1.0 copy-done.8
  83.3 0.9 copy-done.5
  86.0 1.9 fusion.93
  88.7 1.1 copy-done.69
  89.7 1.1 multiply_reduce_fusion.6
  90.9 0.9 fusion.45
  91.8 1.0 fusion.41
  92.8 2.5 %fusion.11 = (bf16[256,2048]{1,0:T(8,128)(2,1)S(1)}, bf16[256,2048]{1,0:T(8,128)(2,1)S(1)}) fusion(f32[256,4096]{1,0:T(8,128)S(1)} %fusion.93, bf16[256,640]{1,0:T(8,128)(2,1)S(1)} %get-tuple-element.70, bf16[2048,640]{1,0:T(8,128)(2,1)S(1)} %bitcast.192), kind=kOutput, calls=%fused_computation.20 | convolution fusion | flops 683671552 | bytes 9240576 | tf_op jit(solution)/shard_map/dot_general | solution.py:51
  95.4 2.5 %multiply_reduce_fusion.2 = (f32[640]{0:T(1024)}, f32[256]{0:T(256)S(1)}, f32[256,640]{1,0:T(8,128)S(1)}) fusion(f32[256,640]{1,0:T(8,128)S(1)} %get-tuple-element.61, f32[256]{0:T(256)S(1)} %fusion.82, f32[640]{0:T(1024)S(1)} %reshape.401, bf16[640,4096]{1,0:T(8,128)(2,1)S(1)} %bitcast.172, bf16[256,2048]{1,0:T(8,128)(2,1)S(1)} %get-tuple-element.63, ...), kind=kOutput, calls=%fused_computation.91 | convolution fusion | flops 1347353728 | bytes 8657920 | tf_op jit(solution)/shard_map/dot_general | solution.py:51
  97.9 1.1 multiply_reduce_fusion.3
  100.5 1.4 convolution_convert_fusion.4
  102.0 2.0 copy.138
  104.0 2.9 %fusion.1 = (f32[4,256]{1,0:T(4,128)S(1)}, f32[768,256,4]{1,0,2:T(8,128)S(1)}) fusion(f32[4,256,768]{1,2,0:T(8,128)} %copy-done.8, f32[4,256]{1,0:T(4,128)S(1)} %copy-done.63, bf16[256,4,256]{0,2,1:T(8,128)(2,1)} %bitcast.183, bf16[768,512]{1,0:T(8,128)(2,1)} %copy-done.14), kind=kOutput, calls=%fused_computation.6 | convolution fusion | flops 405011456 | bytes 7217152 | tf_op jit(solution)/shard_map/qhd,kd->hqk/dot_general | solution.py:649
  111.9 2.5 %convolution_convert_fusion.1 = bf16[2048,640]{1,0:T(8,128)(2,1)} fusion(bf16[256,2048]{1,0:T(8,128)(2,1)S(1)} %copy-done.7, bf16[256,640]{1,0:T(8,128)(2,1)S(1)} %copy-done.20), kind=kOutput, calls=%fused_computation.2 | convolution fusion | flops 672399360 | bytes 3997696 | tf_op jit(solution)/shard_map/dot_general | solution.py:45
  114.4 1.1 fusion.46
  115.5 1.3 collective-permute-start.3
  116.8 1.6 collective-permute-start.2
  119.1 1.2 fusion.18
  120.2 2.1 copy.115
  122.7 2.9 %convolution_convert_fusion.3 = bf16[1024,640]{1,0:T(8,128)(2,1)} fusion(bf16[256,1024]{0,1:T(8,128)(2,1)} %bitcast.177, bf16[256,640]{1,0:T(8,128)(2,1)} %copy-done.17), kind=kOutput, calls=%fused_computation.29 | convolution fusion | flops 336199680 | bytes 2162688 | tf_op jit(solution)/shard_map/dot_general | solution.py:45
  125.6 4.0 %convolution_convert_fusion = bf16[640,4096]{1,0:T(8,128)(2,1)} fusion(bf16[256,2048]{1,0:T(8,128)(2,1)S(1)} %copy-done.24, bf16[256,2048]{1,0:T(8,128)(2,1)S(1)} %copy-done.22, f32[256,640]{1,0:T(8,128)S(1)} %get-tuple-element.61, f32[640]{0:T(1024)S(1)} %reshape.401, f32[256]{0:T(256)S(1)} %fusion.82), kind=kOutput, calls=%fused_computation.1 | convolution fusion | flops 1349484544 | bytes 7998976 | tf_op jit(solution)/shard_map/dot_general | solution.py:45
  129.7 1.3 collective-permute-done.3
  131.1 1.3 fusion.49
  133.6 2.5 %fusion.36 = (f32[640]{0:T(1024)S(1)}, f32[256]{0:T(256)S(1)}, f32[256,640]{1,0:T(8,128)S(1)}) fusion(bf16[1,256,640]{2,1,0:T(8,128)(2,1)S(1)} %copy-done.4, f32[256]{0:T(256)S(1)} %copy-done.57, f32[640]{0:T(1024)S(1)} %copy-done.42, bf16[640,1536]{1,0:T(8,128)(2,1)} %bitcast.179, bf16[256,256]{0,1:T(8,128)(2,1)S(1)} %copy.123, ...), kind=kOutput, calls=%fused_computation.80 | convolution fusion | flops 506821760 | bytes 3742720 | tf_op jit(solution)/shard_map/dot_general | solution.py:51
  136.1 2.2 %convolution_convert_fusion.2 = bf16[640,1536]{1,0:T(8,128)(2,1)} fusion(bf16[1,256,640]{2,1,0:T(8,128)(2,1)S(1)} %copy-done.4, f32[256]{0:T(256)S(1)} %copy-done.57, f32[640]{0:T(1024)S(1)} %copy-done.42, bf16[256,256]{0,1:T(8,128)(2,1)S(1)} %copy.123, bf16[256,256]{0,1:T(8,128)(2,1)S(1)} %copy.122, bf16[256,1024]{0,1:T(8,128)(2,1)S(1)} %bitcast.182), kind=kOutput, calls=%fused_computation.3 | convolution fusion | flops 507314176 | bytes 3083776 | tf_op jit(solution)/shard_map/dot_general | solution.py:45
  139.1 67.3 %reduce_grads.1 = (f32[80,1024]{1,0:T(8,128)}, f32[80,256]{1,0:T(8,128)}, f32[80,256]{1,0:T(8,128)}, f32[128,640]{1,0:T(8,128)}, f32[80,2048]{1,0:T(8,128)}, /*i...) custom-call(bf16[8,80,1536]{2,1,0:T(8,128)(2,1)} %bitcast.180, bf16[8,128,640]{2,1,0:T(8,128)(2,1)} %bitcast.175, ...), custom_call_target="tpu_custom_call" | custom-call | tf_op jit(solution)/shard_map/reduce_grads/pallas_call | solution.py:466
  206.5 1.4 slice_bitcast_fusion.8
  207.8 1.3 slice_bitcast_fusion.6
  209.1 0.9 fusion.52
  212.8 0.8 copy.155
  213.6 0.8 copy.156
  214.5 0.8 copy.157
  (217 shorter events, 22.0 us)
Async XLA Ops:
  0.6 58.8 %copy-start.2 = (bf16[1,256,640]{2,1,0:T(8,128)(2,1)S(1)}, bf16[1,256,640]{2,1,0:T(8,128)(2,1)}, u32[]{:S(2)}) copy-start(bf16[1,256,640]{2,1,0:T(8,128)(2,1)} %param.15) | copy-start | bytes 983044
  0.7 62.2 %copy-start.67 = (f32[128]{0:T(128)}, f32[128]{0:T(128)S(1)}, u32[]{:S(2)}) copy-start(f32[128]{0:T(128)S(1)} %multiply_power_fusion) | copy-start | bytes 1540
  62.2 9.3 %copy-start.64 = (f32[256]{0:T(256)}, f32[256]{0:T(256)S(1)}, u32[]{:S(2)}) copy-start(f32[256]{0:T(256)S(1)} %fusion.84) | copy-start | bytes 3076
  62.8 4.4 %copy-start.48 = (f32[256]{0:T(256)}, f32[256]{0:T(256)S(1)}, u32[]{:S(2)}) copy-start(f32[256]{0:T(256)S(1)} %reshape.398) | copy-start | bytes 3076
  62.8 4.4 %copy-start.50 = (f32[256]{0:T(256)}, f32[256]{0:T(256)S(1)}, u32[]{:S(2)}) copy-start(f32[256]{0:T(256)S(1)} %fusion.80) | copy-start | bytes 3076
  63.5 8.0 %copy-start.32 = (bf16[256,128]{1,0:T(8,128)(2,1)}, bf16[256,128]{1,0:T(8,128)(2,1)S(1)}, u32[]{:S(2)}) copy-start(bf16[256,128]{1,0:T(8,128)(2,1)S(1)} %get-tuple-element.84) | copy-start | bytes 196612
  63.5 8.0 %copy-start.33 = (bf16[256,128]{1,0:T(8,128)(2,1)}, bf16[256,128]{1,0:T(8,128)(2,1)S(1)}, u32[]{:S(2)}) copy-start(bf16[256,128]{1,0:T(8,128)(2,1)S(1)} %get-tuple-element.85) | copy-start | bytes 196612
  64.3 13.4 %collective-permute-start.1 = (bf16[256,512]{1,0:T(8,128)(2,1)}, bf16[256,512]{1,0:T(8,128)(2,1)}, u32[]{:S(2)}, u32[]{:S(2)}) collective-permute-start(bf16[256,512]{1,0:T(8,128)(2,1)} %pad_maximum_fusion.11), channel_id=1, source_target_pairs={{0,8},{8,16},{16,24},{1,9},{9,17},{17,25},{2,10},{10,18},{18,26},{... | collective-permute-start | bytes 786440 | tf_op jit(solution)/shard_map/ppermute | solution.py:20
  67.2 10.4 %collective-permute-start = (bf16[256,512]{1,0:T(8,128)(2,1)}, bf16[256,512]{1,0:T(8,128)(2,1)}, u32[]{:S(2)}, u32[]{:S(2)}) collective-permute-start(bf16[256,512]{1,0:T(8,128)(2,1)} %pad_maximum_fusion.11), channel_id=1, source_target_pairs={{0,16},{8,24},{1,17},{9,25},{2,18},{10,26},{3,19},{11,27},{4,20},{... | collective-permute-start | bytes 786440 | tf_op jit(solution)/shard_map/ppermute | solution.py:20
  70.1 4.4 %copy-start.46 = (f32[256]{0:T(256)}, f32[256]{0:T(256)S(1)}, u32[]{:S(2)}) copy-start(f32[256]{0:T(256)S(1)} %reshape.399) | copy-start | bytes 3076
  71.6 3.9 %copy-start.55 = (f32[8,80]{1,0:T(8,128)S(1)}, f32[8,80]{1,0:T(8,128)}, u32[]{:S(2)}) copy-start(f32[8,80]{1,0:T(8,128)} %get-tuple-element.55) | copy-start | bytes 7684
  71.6 4.0 %copy-start.54 = (f32[8,80]{1,0:T(8,128)S(1)}, f32[8,80]{1,0:T(8,128)}, u32[]{:S(2)}) copy-start(f32[8,80]{1,0:T(8,128)} %get-tuple-element.54) | copy-start | bytes 7684
  79.0 2.8 %copy-start.14 = (bf16[768,512]{1,0:T(8,128)(2,1)}, bf16[768,512]{1,0:T(8,128)(2,1)S(1)}, u32[]{:S(2)}) copy-start(bf16[768,512]{1,0:T(8,128)(2,1)S(1)} %maximum_maximum_fusion) | copy-start | bytes 2359300
  81.7 4.0 %slice-start = ((s8[5242880]{0:T(1024)(128)(4,1)}), s8[4194304]{0:T(1024)(128)(4,1)S(1)}, s32[]{:S(2)}) async-start(s8[5242880]{0:T(1024)(128)(4,1)} %bitcast.169), calls=%async_computation | async-start | bytes 8388608
  81.8 4.3 %slice-start.1 = ((s8[5242880]{0:T(1024)(128)(4,1)}), s8[1048576]{0:T(1024)(128)(4,1)S(1)}, s32[]{:S(2)}) async-start(s8[5242880]{0:T(1024)(128)(4,1)} %bitcast.169), calls=%async_computation.1 | async-start | bytes 2097152
  83.3 4.6 %copy-start.18 = (bf16[256,4,256]{2,0,1:T(8,128)(2,1)}, bf16[256,4,256]{2,0,1:T(8,128)(2,1)S(1)}, u32[]{:S(2)}) copy-start(bf16[256,4,256]{2,0,1:T(8,128)(2,1)S(1)} %convolution_convert_fusion.5) | copy-start | bytes 1572868
  100.5 3.5 %copy-start.63 = (f32[4,256]{1,0:T(4,128)S(1)}, f32[4,256]{1,0:T(4,128)}, u32[]{:S(2)}) copy-start(f32[4,256]{1,0:T(4,128)} %copy-done.62) | copy-start | bytes 12292
  104.0 3.1 %copy-start.9 = (f32[4,256,768]{1,2,0:T(8,128)S(1)}, f32[4,256,768]{1,2,0:T(8,128)}, u32[]{:S(2)}) copy-start(f32[4,256,768]{1,2,0:T(8,128)} %copy-done.8) | copy-start | bytes 9437188
  104.0 3.2 %copy-start.35 = (bf16[256,1024]{0,1:T(8,128)(2,1)S(1)}, bf16[256,1024]{0,1:T(8,128)(2,1)}, u32[]{:S(2)}) copy-start(bf16[256,1024]{0,1:T(8,128)(2,1)} %copy.138) | copy-start | bytes 1572868
  107.8 6.6 %copy-start.10 = (f32[768,256]{1,0:T(8,128)}, f32[768,256]{1,0:T(8,128)S(1)}, u32[]{:S(2)}) copy-start(f32[768,256]{1,0:T(8,128)S(1)} %convolution_bitcast_fusion) | copy-start | bytes 2359300
  110.3 4.1 %copy-start.12 = (f32[768,256]{1,0:T(8,128)}, f32[768,256]{1,0:T(8,128)S(1)}, u32[]{:S(2)}) copy-start(f32[768,256]{1,0:T(8,128)S(1)} %fusion.17) | copy-start | bytes 2359300
  114.4 4.1 %copy-start.47 = (f32[256]{0:T(256)S(1)}, f32[256]{0:T(256)}, u32[]{:S(2)}) copy-start(f32[256]{0:T(256)} %copy-done.46) | copy-start | bytes 3076
  115.5 15.5 %collective-permute-start.3 = (f32[256,512]{1,0:T(8,128)}, f32[256,512]{1,0:T(8,128)}, u32[]{:S(2)}, u32[]{:S(2)}) collective-permute-start(f32[256,512]{1,0:T(8,128)} %get-tuple-element.65), channel_id=1, source_target_pairs={{16,0},{24,8},{17,1},{25,9},{18,2},{26,10},{19,3},{27,11},{20,4},{... | collective-permute-start | bytes 1572872 | tf_op jit(solution)/shard_map/ppermute | solution.py:20
  116.8 14.2 %collective-permute-start.2 = (f32[256,512]{1,0:T(8,128)}, f32[256,512]{1,0:T(8,128)}, u32[]{:S(2)}, u32[]{:S(2)}) collective-permute-start(f32[256,512]{1,0:T(8,128)} %get-tuple-element.64), channel_id=1, source_target_pairs={{8,0},{16,8},{24,16},{9,1},{17,9},{25,17},{10,2},{18,10},{26,18},{... | collective-permute-start | bytes 1572872 | tf_op jit(solution)/shard_map/ppermute | solution.py:20
  119.0 3.4 %copy-start.53 = (f32[640]{0:T(1024)S(1)}, f32[640]{0:T(1024)}, u32[]{:S(2)}) copy-start(f32[640]{0:T(1024)} %get-tuple-element.47) | copy-start | bytes 7684
  119.0 3.4 %copy-start.66 = (f32[640]{0:T(1024)S(1)}, f32[640]{0:T(1024)}, u32[]{:S(2)}) copy-start(f32[640]{0:T(1024)} %get-tuple-element.45) | copy-start | bytes 7684
  119.0 3.5 %copy-start.52 = (f32[640]{0:T(1024)S(1)}, f32[640]{0:T(1024)}, u32[]{:S(2)}) copy-start(f32[640]{0:T(1024)} %get-tuple-element.49) | copy-start | bytes 7684
  120.2 5.4 %copy-start.22 = (bf16[256,2048]{1,0:T(8,128)(2,1)S(1)}, bf16[256,2048]{1,0:T(8,128)(2,1)}, u32[]{:S(2)}) copy-start(bf16[256,2048]{1,0:T(8,128)(2,1)} %copy-done.21) | copy-start | bytes 3145732
  122.7 2.9 %copy-start.24 = (bf16[256,2048]{1,0:T(8,128)(2,1)S(1)}, bf16[256,2048]{1,0:T(8,128)(2,1)}, u32[]{:S(2)}) copy-start(bf16[256,2048]{1,0:T(8,128)(2,1)} %copy-done.23) | copy-start | bytes 3145732
  125.6 5.4 %copy-start.11 = (f32[768,256]{1,0:T(8,128)S(1)}, f32[768,256]{1,0:T(8,128)}, u32[]{:S(2)}) copy-start(f32[768,256]{1,0:T(8,128)} %copy-done.10) | copy-start | bytes 2359300
  125.6 5.4 %copy-start.13 = (f32[768,256]{1,0:T(8,128)S(1)}, f32[768,256]{1,0:T(8,128)}, u32[]{:S(2)}) copy-start(f32[768,256]{1,0:T(8,128)} %copy-done.12) | copy-start | bytes 2359300
  129.7 2.8 %copy-start.68 = (f32[128]{0:T(128)S(1)}, f32[128]{0:T(128)}, u32[]{:S(2)}) copy-start(f32[128]{0:T(128)} %copy-done.67) | copy-start | bytes 1540
  129.7 3.4 %copy-start.49 = (f32[256]{0:T(256)S(1)}, f32[256]{0:T(256)}, u32[]{:S(2)}) copy-start(f32[256]{0:T(256)} %copy-done.48) | copy-start | bytes 3076
  129.7 3.4 %copy-start.51 = (f32[256]{0:T(256)S(1)}, f32[256]{0:T(256)}, u32[]{:S(2)}) copy-start(f32[256]{0:T(256)} %copy-done.50) | copy-start | bytes 3076
  129.7 3.6 %copy-start.61 = (f32[256]{0:T(256)S(1)}, f32[256]{0:T(256)}, u32[]{:S(2)}) copy-start(f32[256]{0:T(256)} %copy-done.60) | copy-start | bytes 3076
  129.7 3.9 %copy-start.4 = (bf16[1,256,640]{2,1,0:T(8,128)(2,1)S(1)}, bf16[1,256,640]{2,1,0:T(8,128)(2,1)}, u32[]{:S(2)}) copy-start(bf16[1,256,640]{2,1,0:T(8,128)(2,1)} %param.15) | copy-start | bytes 983044
  129.7 3.9 %copy-start.34 = (bf16[256,4,256]{0,2,1:T(8,128)(2,1)S(1)}, bf16[256,4,256]{0,2,1:T(8,128)(2,1)}, u32[]{:S(2)}) copy-start(bf16[256,4,256]{0,2,1:T(8,128)(2,1)} %copy.115) | copy-start | bytes 1572868
  129.7 3.9 %copy-start.42 = (f32[640]{0:T(1024)S(1)}, f32[640]{0:T(1024)}, u32[]{:S(2)}) copy-start(f32[640]{0:T(1024)} %copy-done.41) | copy-start | bytes 7684
  129.7 3.9 %copy-start.57 = (f32[256]{0:T(256)S(1)}, f32[256]{0:T(256)}, u32[]{:S(2)}) copy-start(f32[256]{0:T(256)} %copy-done.56) | copy-start | bytes 3076
  139.1 70.0 %copy-start.59 = (f32[256]{0:T(256)S(1)}, f32[256]{0:T(256)}, u32[]{:S(2)}) copy-start(f32[256]{0:T(256)} %copy-done.58) | copy-start | bytes 3076
  139.1 70.0 %copy-start.1 = (f32[256,640]{1,0:T(8,128)S(1)}, f32[256,640]{1,0:T(8,128)}, u32[]{:S(2)}) copy-start(f32[256,640]{1,0:T(8,128)} %copy-done) | copy-start | bytes 1966084
  206.4 3.6 %copy-start.37 = (f32[80,1024]{1,0:T(8,128)S(1)}, f32[80,1024]{1,0:T(8,128)}, u32[]{:S(2)}) copy-start(f32[80,1024]{1,0:T(8,128)} %get-tuple-element.119) | copy-start | bytes 983044
  206.4 4.4 %copy-start.40 = (f32[80,256]{1,0:T(8,128)S(1)}, f32[80,256]{1,0:T(8,128)}, u32[]{:S(2)}) copy-start(f32[80,256]{1,0:T(8,128)} %get-tuple-element.120) | copy-start | bytes 245764
  206.4 5.0 %copy-start.39 = (f32[80,256]{1,0:T(8,128)S(1)}, f32[80,256]{1,0:T(8,128)}, u32[]{:S(2)}) copy-start(f32[80,256]{1,0:T(8,128)} %get-tuple-element.121) | copy-start | bytes 245764
  206.5 5.6 %copy-start.36 = (f32[128,640]{1,0:T(8,128)S(1)}, f32[128,640]{1,0:T(8,128)}, u32[]{:S(2)}) copy-start(f32[128,640]{1,0:T(8,128)} %get-tuple-element.122) | copy-start | bytes 983044
  206.5 6.3 %copy-start.31 = (f32[80,2048]{1,0:T(8,128)S(1)}, f32[80,2048]{1,0:T(8,128)}, u32[]{:S(2)}) copy-start(f32[80,2048]{1,0:T(8,128)} %get-tuple-element.123) | copy-start | bytes 1966084
  209.1 4.5 %copy-start.30 = (f32[80,2048]{1,0:T(8,128)S(1)}, f32[80,2048]{1,0:T(8,128)}, u32[]{:S(2)}) copy-start(f32[80,2048]{1,0:T(8,128)} %get-tuple-element.124) | copy-start | bytes 1966084
  210.1 4.4 %copy-start.29 = (f32[256,640]{1,0:T(8,128)S(1)}, f32[256,640]{1,0:T(8,128)}, u32[]{:S(2)}) copy-start(f32[256,640]{1,0:T(8,128)} %get-tuple-element.125) | copy-start | bytes 1966084
  (28 other events, 50.6 us)
